TPU v7x, 256 devices: a whole 4x4x8 slice. The times are simulated.
256 devices in a mesh: pipe: 16 (over x, z_hi), tensor: 16 (over z_lo, y, core).
Axes of the slice: x: 4, y: 4, z: 8 (z_hi: 4, z_lo: 2; z = z_hi * 2 + z_lo), core: 2. Of those that a mesh axis runs over, the one named last changes fastest.
Arguments:
- hidden_states: bfloat16 [512, 4608], P('tensor'), may hold values from -24 to 24
- embedding: bfloat16 [163840, 4608], P(('pipe', 'tensor')), may hold values from -3 to 3
- token_ids: int32 [512], P('tensor'), may hold values from 0 to 163839
- target_ids: int32 [512], P('tensor'), may hold values from 0 to 163839
- coefficients: bfloat16 [512], P('tensor'), may hold values from -48 to 48
- cotangent: bfloat16 [512, 4608], P('tensor'), may hold values from -0.3125 to 0.3125
- value_weight: bfloat16 [4608], replicated, may hold values from -0.625 to 0.625
- returns: float32 [512], P('tensor'), may hold values from -32 to 32
Outputs:
- grad_embedding: bfloat16 [163840, 4608], P(('pipe', 'tensor'))
- grad_hidden: bfloat16 [512, 4608], P('tensor')
- grad_value: float32 [4608], replicated
All inputs are finite; a program needn't handle non-finite values.
Results may differ from a plain program's by a relative error of at most 0.0034.
Values may be sent and summed in bfloat16 or wider, within the bound.
A program may use at most 128 MiB of HBM per device.

v0:
```python
import math

import jax
import jax.numpy as jnp
from jax import lax
from jax.sharding import PartitionSpec as P

VALUE_SCALE = 0.5


def local(
    hidden_states, embedding, token_ids, target_ids, coefficients, cotangent, value_weight, returns
):
    voc_rows, model_width = embedding.shape
    offset = lax.axis_index(("pipe", "tensor")) * voc_rows
    gathered = (
        lax.all_gather(hidden_states, "tensor", axis=0, tiled=True),
        lax.all_gather(cotangent, "tensor", axis=0, tiled=True),
        lax.all_gather(coefficients, "tensor", axis=0, tiled=True),
        lax.all_gather(token_ids, "tensor", axis=0, tiled=True),
        lax.all_gather(target_ids, "tensor", axis=0, tiled=True),
    )
    every_hidden, every_cotangent, every_coef, every_ids, every_target = gathered
    logits = lax.dot_general(
        every_hidden, embedding, (((1,), (1,)), ((), ())), preferred_element_type=jnp.float32
    )
    local_peak = jnp.max(logits, axis=1)
    row_peak = lax.pmax(local_peak, ("pipe", "tensor"))
    weights = jnp.exp(logits - row_peak[:, None])
    row_total = lax.psum(jnp.sum(weights, axis=1), ("pipe", "tensor"))
    vocab_index = offset + lax.broadcasted_iota(jnp.int32, (1, voc_rows), 1)
    target_hit = (every_target[:, None] == vocab_index).astype(jnp.float32)
    logit_grad = (
        every_coef.astype(jnp.float32)[:, None] * (weights / row_total[:, None] - target_hit)
    ).astype(jnp.bfloat16)
    value_out = jnp.dot(hidden_states, value_weight, preferred_element_type=jnp.float32)
    value_delta = VALUE_SCALE * (value_out - returns)
    value_wide = value_weight.astype(jnp.float32)[None, :]
    tensor_sum = lax.psum_scatter(
        jnp.dot(logit_grad, embedding, preferred_element_type=jnp.float32),
        "tensor",
        scatter_dimension=0,
        tiled=True,
    )
    summed = lax.psum(tensor_sum, "pipe")
    grad_hidden = (summed + value_delta[:, None] * value_wide).astype(jnp.bfloat16)
    local_value = jnp.dot(
        value_delta, hidden_states.astype(jnp.float32), precision=lax.Precision.HIGHEST
    )
    grad_value = lax.psum(local_value, "tensor")
    head_term = lax.dot_general(
        logit_grad, every_hidden, (((0,), (0,)), ((), ())), preferred_element_type=jnp.float32
    )
    normalizer = math.sqrt(model_width)
    lookup_table = (every_ids[:, None] == vocab_index).astype(jnp.bfloat16)
    looked = lax.dot_general(
        lookup_table, every_cotangent, (((0,), (0,)), ((), ())), preferred_element_type=jnp.float32
    )
    grad_embedding = (head_term + normalizer * looked).astype(jnp.bfloat16)
    return (grad_embedding, grad_hidden, grad_value)


def solution(mesh):
    in_specs = (
        P("tensor", None),
        P(("pipe", "tensor"), None),
        P("tensor"),
        P("tensor"),
        P("tensor"),
        P("tensor", None),
        P(),
        P("tensor"),
    )
    out_specs = (P(("pipe", "tensor"), None), P("tensor", None), P())
    return jax.shard_map(local, mesh=mesh, in_specs=in_specs, out_specs=out_specs, check_vma=False)
```

profile of v0, /device:TPU:32, one launch (start us, length us, event | category | flops | bytes accessed | tf_op | source)
XLA Modules:
  0.0 516.7 jit_solution(13293546273978543361)
XLA Ops:
  7.2 0.0 all-gather.3.cloned.1.call-start
  7.2 0.7 all-gather.3.cloned.1.call-update
  7.9 0.0 reduce-scatter.2.cloned.1.call-start
  8.0 1.3 dynamic-slice
  9.9 0.9 dynamic-update-slice
  10.7 29.2 %all-reduce = bf16[512]{0:T(512)(128)(2,1)S(1)} all-reduce(bf16[512]{0:T(512)(128)(2,1)S(1)} %dynamic-update-slice), channel_id=1, replica_groups=mesh['pipe'=16,'tensor'=16] {'tensor'}, use_global_device_ids=true, to_apply=%add | all-reduce | flops 512 | bytes 2048
  40.0 0.9 dynamic-update-slice.1
  40.8 0.8 dynamic-update-slice.2
  41.7 9.2 %all-reduce.3 = (s32[512]{0:T(512)S(1)}, s32[512]{0:T(512)S(1)}) all-reduce(s32[512]{0:T(512)S(1)} %dynamic-update-slice.1, s32[512]{0:T(512)S(1)} %dynamic-update-slice.2), channel_id=1, replica_groups=mesh['pipe'=16,'tensor'=16] {'tensor'}, use_global_device_ids=true, to_apply=%add.1 | all-reduce | flops 1024 | bytes 8192
  50.9 2.2 all-gather.3.cloned.1.call-done
  53.1 7.6 %fusion.9 = (f32[512]{0:T(512)S(1)}, f32[512,640]{1,0:T(8,128)S(1)}) fusion(bf16[512,4608]{1,0:T(8,128)(2,1)} %all-gather.3.cloned.1.call-done, bf16[640,4608]{1,0:T(8,128)(2,1)} %param.9), kind=kOutput, calls=%fused_computation.16 | convolution fusion | flops 3020226048 | bytes 11929600 | tf_op jit(solution)/shard_map/dot_general | solution.py:24
  60.7 77.3 %pmax.7 = f32[512]{0:T(512)S(1)} all-reduce(f32[512]{0:T(512)S(1)} %get-tuple-element.5), channel_id=1, replica_groups=mesh['pipe'=16,'tensor'=16] {'pipe','tensor'}, use_global_device_ids=true, to_apply=%region_1.0 | all-reduce | flops 512 | bytes 4096 | tf_op jit(solution)/shard_map/pmax | solution.py:28
  138.0 0.3 fusion.1
  138.3 73.7 %psum.21 = f32[512]{0:T(512)S(1)} all-reduce(f32[512]{0:T(512)S(1)} %fusion.1), channel_id=1, replica_groups=mesh['pipe'=16,'tensor'=16] {'pipe','tensor'}, use_global_device_ids=true, to_apply=%region_3.0 | all-reduce | flops 512 | bytes 4096 | tf_op jit(solution)/shard_map/psum | solution.py:30
  212.1 9.2 %fusion.7 = f32[512,4608]{1,0:T(8,128)} fusion(bf16[640,4608]{1,0:T(8,128)(2,1)} %param.9, f32[512,640]{1,0:T(8,128)S(1)} %get-tuple-element.6, s32[640]{0:T(1024)S(1)} %iota_add_fusion, f32[512]{0:T(512)S(1)} %psum.21, f32[512]{0:T(512)S(1)} %pmax.7, f32[512]{0:T(512)S(1)} %convert_element_type.20, s32[512]{0:T(512)S(1)} %get-tuple-element.3), kind=kOutput, calls=%fused_computation.14 | convolution fusion | flops 3022192640 | bytes 16656896 | tf_op jit(solution)/shard_map/dot_general | solution.py:40
  221.2 0.0 reduce-scatter.2.cloned.1.call-update
  221.3 0.0 all-gather.5.cloned.1.call-start
  221.3 0.7 all-gather.5.cloned.1.call-update
  222.0 0.0 all-reduce.6.cloned.1.call-start
  222.0 0.0 copy-done.1
  222.1 0.1 copy-done
  222.2 0.0 copy-done.2
  222.2 0.2 fusion.3
  222.4 0.3 convolution_reduce_fusion
  222.7 55.1 %psum.23 = f32[4608]{0:T(1024)} all-reduce(f32[4608]{0:T(1024)S(1)} %convolution_reduce_fusion), channel_id=1, replica_groups=mesh['pipe'=16,'tensor'=16] {'tensor'}, use_global_device_ids=true, to_apply=%region_6.0 | all-reduce | flops 4608 | bytes 36864 | tf_op jit(solution)/shard_map/psum | solution.py:50
  277.7 10.4 %fusion.8 = f32[640,4608]{1,0:T(8,128)} fusion(bf16[512,4608]{1,0:T(8,128)(2,1)} %all-gather.3.cloned.1.call-done, f32[512,640]{1,0:T(8,128)S(1)} %get-tuple-element.6, s32[640]{0:T(1024)S(1)} %iota_add_fusion, f32[512]{0:T(512)S(1)} %psum.21, f32[512]{0:T(512)S(1)} %pmax.7, f32[512]{0:T(512)S(1)} %convert_element_type.20, s32[512]{0:T(512)S(1)} %get-tuple-element.3), kind=kOutput, calls=%fused_computation.15 | convolution fusion | flops 3022192640 | bytes 17836544 | tf_op jit(solution)/shard_map/dot_general | solution.py:51
  288.1 7.8 %reduce-scatter.2.cloned.1.call-done = f32[32,4608]{1,0:T(8,128)} async-done(((f32[512,4608]{1,0:T(8,128)}), f32[32,4608]{1,0:T(8,128)}) %reduce-scatter.2.cloned.1.call-update) | async-done | bytes 589840 | tf_op jit(solution)/shard_map/reduce_scatter | solution.py:39
  295.9 0.0 all-reduce.6.cloned.1.call-update
  295.9 42.2 %all-gather.5.cloned.1.call-done = bf16[512,4608]{1,0:T(8,128)(2,1)} async-done(((bf16[32,4608]{1,0:T(8,128)(2,1)}), bf16[512,4608]{1,0:T(8,128)(2,1)}) %all-gather.5.cloned.1.call-update) | async-done | bytes 4718608 | tf_op jit(solution)/shard_map/all_gather | solution.py:18
  338.1 11.8 %add_convert_fusion = bf16[640,4608]{1,0:T(8,128)(2,1)} fusion(f32[640,4608]{1,0:T(8,128)} %fusion.8, bf16[512,4608]{1,0:T(8,128)(2,1)} %all-gather.5.cloned.1.call-done, s32[640]{0:T(1024)S(1)} %iota_add_fusion, s32[512]{0:T(512)S(1)} %get-tuple-element.4), kind=kOutput, calls=%fused_computation | convolution fusion | flops 3029073920 | bytes 22417920 | tf_op jit(solution)/shard_map/dot_general | solution.py:56
  349.9 158.4 %all-reduce.6.cloned.1.call-done = f32[32,4608]{1,0:T(8,128)} async-done(((f32[32,4608]{1,0:T(8,128)}), f32[32,4608]{1,0:T(8,128)}) %all-reduce.6.cloned.1.call-update) | async-done | bytes 589840 | tf_op jit(solution)/shard_map/psum | solution.py:45
  508.3 1.9 add_convert_fusion.1
  (10 shorter events, 0.0 us)
Async XLA Ops:
  7.2 45.9 %all-gather.3.cloned.1.call-start = ((), (), s32[]{:S(2)}) async-start(), calls=%async_computation.1 | async-start | bytes 5013504 | tf_op jit(solution)/shard_map/all_gather | solution.py:17
  7.9 288.0 %reduce-scatter.2.cloned.1.call-start = ((), (), s32[]{:S(2)}) async-start(), calls=%async_computation.3 | async-start | bytes 10027008 | tf_op jit(solution)/shard_map/reduce_scatter | solution.py:39
  221.2 0.8 copy-start.1
  221.2 1.0 copy-start
  221.2 1.0 copy-start.2
  221.3 116.9 %all-gather.5.cloned.1.call-start = ((), (), s32[]{:S(2)}) async-start(), calls=%async_computation.2 | async-start | bytes 5013504 | tf_op jit(solution)/shard_map/all_gather | solution.py:18
  222.0 286.3 %all-reduce.6.cloned.1.call-start = ((), (), s32[]{:S(2)}) async-start(), calls=%async_computation.4 | async-start | bytes 1179648 | tf_op jit(solution)/shard_map/psum | solution.py:45
Sparse Core Ops, SparseCore 0:
  9.8 43.2 all-gather.2
  221.4 74.4 reduce-scatter.1
  297.7 40.3 all-gather.4
  340.6 167.5 all-reduce.5
where the time goes:
time: 519 us; the launch traced here: 517 us
  blocking collectives  244 us (47%)
  waiting for transfers between devices  212 us (41%)
  matrix products  39.3 us (8%)
  between operations  14.5 us (3%)
    psum x1, waiting for transfers between devices, local(): summed = lax.psum(tensor_sum, 'pipe')  158 us
    pmax x1, blocking collectives, local(): row_peak = lax.pmax(local_peak, ('pipe', 'tensor'))  77.3 us
    psum x1, blocking collectives, local(): row_total = lax.psum(jnp.sum(weights, axis=1), ('pipe', 'tensor'))  73.7 us
    psum x1, blocking collectives, local(): grad_value = lax.psum(local_value, 'tensor')  55.1 us
    all_gather x1, waiting for transfers between devices, local(): lax.all_gather(cotangent, 'tensor', axis=0, tiled=True)  42.2 us
    unnamed x2, blocking collectives  38.4 us
    dot_general x1, matrix products, local(): lax.dot_general(lookup_table, every_cotangent, (((0,), (0,)), ((), ())),...  11.8 us
  transfers between devices with their start and end apart: 4, of which 4 were waited for; matrix products, arithmetic and copies ran while one was open for 5% of the time, Pallas kernels for 0%

commit v1 on v0

v1 whole, which is shorter than its diff:
```python
import math

import jax
import jax.numpy as jnp
from jax import lax
from jax.experimental import pallas as pl
from jax.experimental.pallas import tpu as pltpu
from jax.sharding import PartitionSpec as P

VALUE_SCALE = 0.5
MESH = pl.DeviceIdType.MESH
F32, BF16 = jnp.float32, jnp.bfloat16

ROWS = 32
TOK = 512
D = 4608
HALF = D // 2
PIECE = 768
QUART = PIECE // 2
VOC = 640
W = HALF // 2
SENDS = 224


def align(value, to=128):
    return pl.multiple_of(value, to)


def kernel(
    hs, emb, tid, tgt, coef, cot, vw, ret,
    ge, gh, gv,
    H, C, E, EH, LT, GS, GT, PA, PB, SA, SB, RA, RB, SA2, SB2, RA2, RB2,
    ZS, ZR, FZ, OUT, META, STA, RSA, STB, RSB, VB, VR, GO,
    ss, rs, ls, xs,
):
    pipe, tensor = lax.axis_index("pipe"), lax.axis_index("tensor")
    x, zh = pipe // 4, pipe % 4
    zl, y, c = tensor // 8, (tensor // 2) % 4, tensor % 2
    z = 2 * zh + zl
    q = x % 2

    def dev(dx=0, dy=0, dz=0, dc=0):
        xx, yy, zz, cc = (x + dx) % 4, (y + dy) % 4, (z + dz + 8) % 8, (c + dc) % 2
        return xx * 4 + zz // 2, (zz % 2) * 8 + yy * 2 + cc

    pair = 1 - 2 * zl

    counter = [0]
    started = []

    def send(src, dst, target):
        k = counter[0]
        counter[0] += 1
        cp = pltpu.make_async_remote_copy(
            src_ref=src, dst_ref=dst, send_sem=ss.at[k], recv_sem=rs.at[k],
            device_id=target, device_id_type=MESH,
        )
        cp.start()
        started.append(cp)
        return cp

    def load(src, dst, k):
        cp = pltpu.make_async_copy(src, dst, ls.at[k])
        cp.start()
        return cp

    my_half = pl.ds(align(c * HALF), HALF)
    sib_half = pl.ds(align((1 - c) * HALF), HALF)
    ld_h = load(hs, H.at[0, 0, 0], 0)
    ld_e = load(emb, E, 1)
    ld_c = load(cot, C.at[0, 0, 0], 2)
    ld_eh = load(emb.at[:, my_half], EH.at[0:VOC], 3)

    plane = [(dx, dy) for dx in range(4) for dy in range(4) if (dx, dy) != (0, 0)]
    column = [(dz, dc) for dz in range(8) for dc in range(2) if (dz, dc) != (0, 0)]
    peers = [(dx, dy, 0, 0) for dx, dy in plane] + [(0, 0, dz, dc) for dz, dc in column]
    peers += [(dx, 0, 0, 1) for dx in (1, 2, 3)]
    bar = pltpu.get_barrier_semaphore()
    for peer in peers:
        pl.semaphore_signal(bar, inc=1, device_id=dev(*peer), device_id_type=MESH)

    META[0, 0, 0] = jnp.zeros((8, 128), F32)
    META[0, 0, 0, 0:1, 0:ROWS] = tid[...].astype(F32)
    META[0, 0, 0, 1:2, 0:ROWS] = tgt[...].astype(F32)
    META[0, 0, 0, 2:3, 0:ROWS] = coef[...].astype(F32)
    pl.semaphore_wait(bar, len(peers))

    def cols(half, j):
        return pl.ds(align(half * HALF + j * PIECE), PIECE)

    def quarter(half, j, k):
        return pl.ds(align(half * HALF + j * PIECE + k * QUART), QUART)

    class Gather:
        def __init__(self, X):
            self.X = X
            self.m = {}

        def begin(self):
            X, m = self.X, self.m
            for j in range(3):
                m["za", j] = send(X.at[0, 0, 0, :, cols(q, j)], X.at[0, 1, 0, :, cols(q, j)], dev(dz=1))
                self.ysend(0, j)
                m["zb", j] = send(X.at[0, 0, 0, :, cols(1 - q, j)], X.at[0, 1, 0, :, cols(1 - q, j)], dev(dz=-1))
                if j == 0:
                    m["s0"] = send(X.at[0, 0, 0], X.at[0, 0, 1], dev(dc=1))

        def ysend(self, dz, j):
            X, m = self.X, self.m
            for dy in (1, 3, 2):
                part = X.at[0, dz, 0, :, cols(q, j)]
                m["y", dz, dy, j] = send(part, X.at[dy, dz, 0, :, cols(q, j)], dev(dy=-dy))

        def s1(self, j):
            X, m = self.X, self.m
            m["za", j].wait_recv()
            self.ysend(1, j)
            m["zb", j].wait_recv()
            for h, k in ((q, "sza"), (1 - q, "szb")):
                m[k, j] = send(X.at[0, 1, 0, :, cols(h, j)], X.at[0, 1, 1, :, cols(h, j)], dev(dc=1))

        def relay(self, dz, j):
            X, m = self.X, self.m
            for dy in (1, 2, 3):
                m["y", dz, dy, j].wait_recv()
            rows = pl.ds(1, 3)
            for k, dx in ((0, 1), (1, -1)):
                part = X.at[rows, dz, 0, :, quarter(q, j, k)]
                m["x", dz, k, j] = counter[0]
                send(part, part, dev(dx=dx))
            m["sy", dz, j] = send(
                X.at[rows, dz, 0, :, cols(q, j)], X.at[rows, dz, 1, :, cols(q, j)], dev(dc=1)
            )

        def s4(self, j):
            X, m = self.X, self.m
            rows = pl.ds(1, 3)
            for dz in range(2):
                for k in range(2):
                    part = X.at[rows, dz, 0, :, quarter(1 - q, j, k)]
                    pltpu.make_async_remote_copy(
                        src_ref=part, dst_ref=part, send_sem=ss.at[m["x", dz, k, j]],
                        recv_sem=rs.at[m["x", dz, k, j]], device_id=dev(dc=1), device_id_type=MESH,
                    ).wait_recv()
                m["sx", dz, j] = send(
                    X.at[rows, dz, 0, :, cols(1 - q, j)], X.at[rows, dz, 1, :, cols(1 - q, j)], dev(dc=1)
                )

        def s5(self, j):
            m = self.m
            if j == 0:
                m["s0"].wait_recv()
            for k in ("sza", "szb"):
                m[k, j].wait_recv()
            for dz in range(2):
                m["sy", dz, j].wait_recv()
                m["sx", dz, j].wait_recv()

    gat_h, gat_c = Gather(H), Gather(C)

    ld_h.wait()
    gat_h.begin()

    h_own = H[0, 0, 0].astype(F32)
    value_out = jnp.sum(h_own * vw[...].astype(F32), axis=1, keepdims=True)
    eye = lax.broadcasted_iota(jnp.int32, (ROWS, ROWS), 0) == lax.broadcasted_iota(jnp.int32, (ROWS, ROWS), 1)
    ret_col = jnp.sum(jnp.where(eye, jnp.broadcast_to(ret[...], (ROWS, ROWS)), 0.0), axis=1, keepdims=True)
    delta = VALUE_SCALE * (value_out - ret_col)
    META[0, 0, 0, 3:4, 0:ROWS] = jnp.sum(jnp.where(eye, delta, 0.0), axis=0, keepdims=True)
    VB[0] = jnp.sum(delta * h_own, axis=0, keepdims=True)
    me_s = send(META.at[0, 0, 0], META.at[0, 0, 1], dev(dc=1))
    vv = [send(VB.at[0], VR.at[0], dev(dc=1))]

    gat_h.s1(0)
    gat_h.relay(0, 0)
    ld_e.wait()
    eh_s = send(E.at[:, sib_half], EH.at[VOC : 2 * VOC], dev(dc=1))
    gat_h.s1(1)
    gat_h.relay(1, 0)
    gat_h.relay(0, 1)
    me_s.wait_recv()
    me_z = send(META.at[0, 0], META.at[0, 1], dev(dz=pair))
    gat_h.s1(2)
    gat_h.relay(1, 1)
    gat_h.s4(0)
    gat_h.relay(0, 2)
    me_z.wait_recv()
    me_y = [send(META.at[0], META.at[dy], dev(dy=-dy)) for dy in (1, 2, 3)]
    vv[0].wait_recv()

    def value_step(k, target):
        VB[k] = VB[k - 1] + VR[k - 1]
        vv.append(send(VB.at[k], VR.at[k], target))

    value_step(1, dev(dz=pair))
    gat_h.s5(0)

    def logits(j):
        def tile(n, _):
            total = jnp.zeros((VOC, 256), F32)
            for half in range(2):
                at = half * HALF + j * PIECE
                rows = H[pl.ds(2 * n, 2), :, :, :, at : at + PIECE].reshape(256, PIECE)
                total += lax.dot_general(
                    E[:, at : at + PIECE], rows, (((1,), (1,)), ((), ())), preferred_element_type=F32
                )
            where = (slice(None), pl.ds(align(n * 256, 256), 256))
            LT[where] = total if j == 0 else LT[where] + total
            return 0

        lax.fori_loop(0, 2, tile, 0)

    logits(0)
    gat_h.relay(1, 2)
    gat_h.s4(1)
    ld_c.wait()
    gat_c.begin()
    gat_h.s5(1)
    logits(1)
    gat_h.s4(2)
    vv[1].wait_recv()
    value_step(2, dev(dy=1 - 2 * (y % 2)))
    gat_h.s5(2)
    logits(2)

    peak = jnp.max(LT[...], axis=0, keepdims=True)
    total = jnp.sum(jnp.exp(LT[...] - peak), axis=0, keepdims=True)
    STA[0:1] = peak
    STA[1:2] = total
    sta = {}
    for dx, dy in plane:
        back = (-dx % 4) * 4 + (-dy % 4)
        sta[back] = send(STA, RSA.at[back], dev(dx=dx, dy=dy))

    def merge(stats):
        peaks = stats[0][0]
        for p, _ in stats[1:]:
            peaks = jnp.maximum(peaks, p)
        sums = sum(s * jnp.exp(p - peaks) for p, s in stats)
        return peaks, sums

    gat_c.s1(0)
    gat_c.relay(0, 0)

    stats = [(peak, total)]
    for dx, dy in plane:
        k = dx * 4 + dy
        sta[k].wait_recv()
        got = RSA[k]
        if dy:
            got = jnp.concatenate([got[:, 128 * (4 - dy) :], got[:, : 128 * (4 - dy)]], axis=1)
        stats.append((got[0:1], got[1:2]))
    peak, total = merge(stats)
    STB[0:1] = peak
    STB[1:2] = total
    stb = {}
    for dz, dc in column:
        back = (-dz % 8) * 2 + dc
        stb[back] = send(STB, RSB.at[back], dev(dz=dz, dc=dc))

    gat_c.s1(1)
    gat_c.relay(1, 0)

    lane = lax.broadcasted_iota(jnp.int32, (2, 128), 1)

    def reorder(p, s, odd, dc):
        both = jnp.concatenate([p, s], axis=0)
        groups = []
        for g in range(4):
            part = both[:, 128 * g : 128 * (g + 1)]
            if odd:
                part = pltpu.roll(part, 64, 1)
            if dc:
                part = jnp.where((lane // 32) % 2 == 0, pltpu.roll(part, 96, 1), pltpu.roll(part, 32, 1))
            groups.append(part)
        both = jnp.concatenate(groups, axis=1)
        return both[0:1], both[1:2]

    classes = []
    for odd in range(2):
        for dc in range(2):
            stats = []
            for dz in range(odd, 8, 2):
                k = dz * 2 + dc
                if k == 0:
                    stats.append((peak, total))
                    continue
                stb[k].wait_recv()
                got = RSB[k]
                stats.append((got[0:1], got[1:2]))
            classes.append(reorder(*merge(stats), odd, dc))
    peak, total = merge(classes)

    for cp in me_y:
        cp.wait_recv()

    def facts():
        groups = []
        for dy in range(4):
            part = META[dy, 0, 0]
            for k in range(1, 4):
                part = part + pltpu.roll(META[dy, k // 2, k % 2], 32 * k, 1)
            groups.append(part)
        return jnp.concatenate(groups, axis=1)

    fact = facts()
    offset = (pipe * 16 + tensor) * VOC
    coefs, target, token = fact[2:3], fact[1:2], fact[0:1]
    inverse = 1.0 / total

    for i in range(5):
        rows = pl.ds(i * 128, 128)
        vocab = (offset + i * 128 + lax.broadcasted_iota(jnp.int32, (128, 1), 0)).astype(F32)
        hit = (target == vocab).astype(F32)
        grad = coefs * (jnp.exp(LT[rows, :] - peak) * inverse - hit)
        GS[rows, :] = grad.astype(BF16)
        turned = grad.T.astype(BF16)
        GT[:, :, :, :, i * 128 : (i + 1) * 128] = turned.reshape(4, 2, 2, ROWS, 128)
    gts = [
        send(GT.at[:, :, k, :, 0:VOC], GT.at[:, :, 1 - k, :, VOC : 2 * VOC], dev(dc=1)) for k in range(2)
    ]
    eh_s.wait_recv()
    ld_eh.wait()
    for cp in gts:
        cp.wait_recv()

    def partial(full, halves, base):
        def tile(n, _):
            at = pl.ds(align(n * QUART), QUART)
            got = jnp.dot(
                GT[...].reshape(TOK, 2 * VOC), EH[:, pl.ds(align(base + n * QUART), QUART)],
                preferred_element_type=F32,
            ).reshape(4, 2, 2, ROWS, QUART)
            full[..., at] = got[: full.shape[0]]
            halves[..., at] = got.astype(BF16)
            return 0

        lax.fori_loop(0, W // QUART, tile, 0)

    def block_of(dx):
        xx = (x + dx) % 4
        return (xx // 2 + zl) % 2, (xx % 2 + c) % 2

    partial(PA, SA, 0)
    ra = [send(SA.at[dy], RA.at[dy - 1], dev(dy=dy)) for dy in (1, 3, 2)]
    partial(PB, SB, W)
    rb = []
    for dx in (1, 3, 2):
        dz, dc = block_of(dx)
        rb.append(send(SB.at[:, dz, dc], RB.at[dx - 1], dev(dx=dx)))

    gat_c.relay(0, 1)
    gat_c.s1(2)
    gat_c.relay(1, 1)
    gat_c.s4(0)
    gat_c.relay(0, 2)
    gat_c.relay(1, 2)
    gat_c.s4(1)
    gat_c.s4(2)
    vv[2].wait_recv()
    value_step(3, dev(dy=2))
    for j in range(3):
        gat_c.s5(j)

    vocab = (offset + lax.broadcasted_iota(jnp.int32, (VOC, 1), 0)).astype(F32)
    LK = (token == vocab).astype(BF16)
    LT[...] = jnp.zeros_like(LT)
    normalizer = math.sqrt(D)
    outs = []
    for n in range(6):
        at = slice(n * PIECE, (n + 1) * PIECE)
        head = jnp.dot(GS[...], H[:, :, :, :, at].reshape(TOK, PIECE), preferred_element_type=F32)
        looked = jnp.dot(LK, C[:, :, :, :, at].reshape(TOK, PIECE), preferred_element_type=F32)
        if n >= 2:
            outs[n - 2].wait()
        GO[n % 2] = (head + normalizer * looked).astype(BF16)
        outs.append(load(GO.at[n % 2], ge.at[:, at], 4 + n))

    for cp in ra:
        cp.wait_recv()
    sum_a = PA[0]
    for k in range(3):
        sum_a += RA[k].astype(F32)
    PA[0] = sum_a
    SA2[...] = sum_a.astype(BF16)
    ra2 = []
    for dx in (1, 3, 2):
        dz, dc = block_of(dx)
        ra2.append(send(SA2.at[dz, dc], RA2.at[dx - 1], dev(dx=dx)))
    dz0, dc0 = block_of(0)
    for cp in rb:
        cp.wait_recv()
    sum_b = PB[:, dz0, dc0]
    for k in range(3):
        sum_b += RB[k].astype(F32)
    SB2[...] = sum_b.astype(BF16)
    rb2 = [send(SB2.at[dy], RB2.at[dy - 1], dev(dy=dy)) for dy in (1, 3, 2)]
    for cp in ra2:
        cp.wait_recv()
    fin_a = PA[0, dz0, dc0]
    for k in range(3):
        fin_a += RA2[k].astype(F32)
    ZS[0] = fin_a.astype(BF16).reshape(2, 16, W)
    for cp in rb2:
        cp.wait_recv()
    fin_b = sum_b[0]
    for k in range(3):
        fin_b += RB2[k].astype(F32)
    ZS[1] = fin_b.astype(BF16).reshape(2, 16, W)

    away = (x // 2 + zl) % 2
    zk = counter[0]
    counter[0] += 8

    def z_copy(k):
        zz = (z + away + 2 * k) % 8
        piece = zz // 2
        slot = away * 4 + k
        return pltpu.make_async_remote_copy(
            src_ref=ZS.at[piece // 2, piece % 2], dst_ref=ZR.at[slot], send_sem=ss.at[zk + k],
            recv_sem=rs.at[zk + slot], device_id=dev(dz=away + 2 * k), device_id_type=MESH,
        )

    for k in range(1, 4):
        z_copy(k).start()

    @pl.when(away == 1)
    def _():
        z_copy(0).start()

    gk = counter[0]
    counter[0] += 3
    ok = counter[0]
    counter[0] += 4

    def g_copy(k):
        return pltpu.make_async_remote_copy(
            src_ref=FZ.at[zh // 2, zh % 2], dst_ref=FZ.at[zh // 2, zh % 2], send_sem=ss.at[gk + k - 1],
            recv_sem=rs.at[gk + k - 1], device_id=dev(dz=2 * k), device_id_type=MESH,
        )

    tok_core = x % 2

    def o_copy(dx):
        xx = (x + dx) % 4
        return pltpu.make_async_remote_copy(
            src_ref=FZ, dst_ref=OUT.at[c], send_sem=ss.at[ok + dx], recv_sem=rs.at[ok + c],
            device_id=(xx * 4 + zh, zl * 8 + y * 2 + tok_core), device_id_type=MESH,
        )

    @pl.when(away == 0)
    def _():
        for slot in range(1, 8):
            pltpu.make_async_remote_copy(
                src_ref=ZR.at[slot], dst_ref=ZR.at[slot], send_sem=ss.at[zk], recv_sem=rs.at[zk + slot],
                device_id=dev(dz=1), device_id_type=MESH,
            ).wait_recv()
        ab, rh = zh // 2, zh % 2
        acc = ZS[ab, rh].astype(F32)
        for slot in range(1, 8):
            acc += ZR[slot].astype(F32)
        row = META[0, 0, dc0, 3:4, :]
        lanes = lax.broadcasted_iota(jnp.int32, (16, 128), 1)
        picks = lanes == lax.broadcasted_iota(jnp.int32, (16, 128), 0) + 16 * rh
        delta16 = jnp.sum(jnp.where(picks, row, 0.0), axis=1, keepdims=True)
        wide = vw[:, pl.ds(align(c * HALF + ab * W), W)].astype(F32)
        FZ[ab, rh] = (acc + delta16 * wide).astype(BF16)
        for k in range(1, 4):
            g_copy(k).start()
        for k in range(1, 4):
            piece = (zh - k + 4) % 4
            part = FZ.at[piece // 2, piece % 2]
            pltpu.make_async_remote_copy(
                src_ref=part, dst_ref=part, send_sem=ss.at[gk], recv_sem=rs.at[gk + k - 1],
                device_id=dev(dz=2), device_id_type=MESH,
            ).wait_recv()
        for dx in (1, 3, 2):
            o_copy(dx).start()

        @pl.when(tok_core == c)
        def _():
            local = pltpu.make_async_copy(FZ, OUT.at[c], xs.at[0])
            local.start()
            local.wait()

        @pl.when(tok_core != c)
        def _():
            o_copy(0).start()

    vv[3].wait_recv()
    gv[...] = VB[3] + VR[3]

    def o_wait(core):
        pltpu.make_async_remote_copy(
            src_ref=FZ, dst_ref=OUT.at[core], send_sem=ss.at[ok], recv_sem=rs.at[ok + core],
            device_id=dev(dx=1), device_id_type=MESH,
        ).wait_recv()

    home = (zl * 2 + c) == x
    o_wait(1 - c)

    @pl.when(jnp.logical_not(home))
    def _():
        o_wait(c)

    for cs in range(2):
        for ab in range(2):
            at = cs * HALF + ab * W
            for rh in range(2):
                gh[rh * 16 : (rh + 1) * 16, at : at + W] = OUT[cs, ab, rh]

    assert counter[0] <= SENDS, counter[0]
    for cp in started:
        cp.wait_send()
    for k in range(1, 4):
        z_copy(k).wait_send()

    @pl.when(away == 1)
    def _():
        z_copy(0).wait_send()

    @pl.when(away == 0)
    def _():
        for k in range(1, 4):
            g_copy(k).wait_send()
        for dx in (1, 3, 2):
            o_copy(dx).wait_send()

        @pl.when(tok_core != c)
        def _():
            o_copy(0).wait_send()

    for cp in outs[-2:]:
        cp.wait()


def local(hidden_states, embedding, token_ids, target_ids, coefficients, cotangent, value_weight, returns):
    vmem, anywhere = pl.BlockSpec(memory_space=pltpu.VMEM), pl.BlockSpec(memory_space=pl.ANY)
    V, dma = pltpu.VMEM, pltpu.SemaphoreType.DMA
    ge, gh, gv = pl.pallas_call(
        kernel,
        out_shape=(
            jax.ShapeDtypeStruct((VOC, D), BF16),
            jax.ShapeDtypeStruct((ROWS, D), BF16),
            jax.ShapeDtypeStruct((1, D), F32),
        ),
        in_specs=[anywhere, anywhere, vmem, vmem, vmem, anywhere, vmem, vmem],
        out_specs=(anywhere, vmem, vmem),
        scratch_shapes=[
            V((4, 2, 2, ROWS, D), BF16),
            V((4, 2, 2, ROWS, D), BF16),
            V((VOC, D), BF16),
            V((2 * VOC, HALF), BF16),
            V((VOC, TOK), F32),
            V((VOC, TOK), BF16),
            V((4, 2, 2, ROWS, 2 * VOC), BF16),
            V((1, 2, 2, ROWS, W), F32),
            V((4, 2, 2, ROWS, W), F32),
            V((4, 2, 2, ROWS, W), BF16),
            V((4, 2, 2, ROWS, W), BF16),
            V((3, 2, 2, ROWS, W), BF16),
            V((3, 4, ROWS, W), BF16),
            V((2, 2, ROWS, W), BF16),
            V((4, ROWS, W), BF16),
            V((3, ROWS, W), BF16),
            V((3, ROWS, W), BF16),
            V((2, 2, 16, W), BF16),
            V((8, 16, W), BF16),
            V((2, 2, 16, W), BF16),
            V((2, 2, 2, 16, W), BF16),
            V((4, 2, 2, 8, 128), F32),
            V((2, TOK), F32),
            V((16, 2, TOK), F32),
            V((2, TOK), F32),
            V((16, 2, TOK), F32),
            V((4, 1, D), F32),
            V((4, 1, D), F32),
            V((2, VOC, PIECE), BF16),
            dma((SENDS,)),
            dma((SENDS,)),
            dma((10,)),
            dma((1,)),
        ],
        compiler_params=pltpu.CompilerParams(
            collective_id=0, has_side_effects=True, vmem_limit_bytes=60 << 20
        ),
        name="policy_head",
    )(
        hidden_states, embedding, token_ids.reshape(1, ROWS), target_ids.reshape(1, ROWS),
        coefficients.reshape(1, ROWS), cotangent, value_weight.reshape(1, D), returns.reshape(1, ROWS),
    )
    return ge, gh, gv.reshape(D)


def solution(mesh):
    in_specs = (
        P("tensor", None),
        P(("pipe", "tensor"), None),
        P("tensor"),
        P("tensor"),
        P("tensor"),
        P("tensor", None),
        P(),
        P("tensor"),
    )
    out_specs = (P(("pipe", "tensor"), None), P("tensor", None), P())
    return jax.shard_map(local, mesh=mesh, in_specs=in_specs, out_specs=out_specs, check_vma=False)
```

time: 519 us -> 124 us (0.24)
  blocking collectives: 244 us -> 0 us
  waiting for transfers between devices: 212 us -> 0 us
  Pallas kernels: 0 us -> 114 us
  matrix products: 39.3 us -> 0 us
  between operations: 14.5 us -> 0.64 us
    psum x1 -> x0, waiting for transfers between devices: 158 us -> none  [local(): summed = lax.psum(tensor_sum, 'pipe')]
    psum x2 -> x0, blocking collectives: 129 us -> none  [the longest x1 73.7 us: local(): row_total = lax.psum(jnp.sum(weights, axis=1), ('pipe', 'tensor'))]
    pallas_call x0 -> x1, Pallas kernels: none -> 114 us  [local(): pl.pallas_call(kernel, out_shape=(jax.ShapeDtypeStruct((VOC, D), BF16), j...]
    pmax x1 -> x0, blocking collectives: 77.3 us -> none  [local(): row_peak = lax.pmax(local_peak, ('pipe', 'tensor'))]
    all_gather x2 -> x0, waiting for transfers between devices: 44.5 us -> none  [the longest x1 42.2 us: local(): lax.all_gather(cotangent, 'tensor', axis=0, tiled=True)]
    dot_general x6 -> x0, matrix products: 39.3 us -> none  [the longest x1 11.8 us: local(): lax.dot_general(lookup_table, every_cotangent, (((0,), (0,)), ((), ())),...]
    unnamed x2 -> x0, blocking collectives: 38.4 us -> none
    reduce_scatter x1 -> x0, waiting for transfers between devices: 7.81 us -> none  [local(): lax.psum_scatter(jnp.dot(logit_grad, embedding, preferred_element_type=jn...]
  transfers between devices with their start and end apart: 4 -> 0, of which waited for: 4 -> 0; matrix products, arithmetic and copies ran while one was open for 5% -> 0% of each run, Pallas kernels for 0% -> 0%
where the time goes in v1:
time: 124 us
  Pallas kernels  114 us (92%)
  local copies, waits for them, and re-layouts  7.71 us (6%)
  other arithmetic  1.38 us (1%)
    pallas_call x1, Pallas kernels, local(): pl.pallas_call(kernel, out_shape=(jax.ShapeDtypeStruct((VOC, D), BF16), j...  114 us
    unnamed x4, local copies, waits for them, and re-layouts  6.39 us

profile of v1, /device:TPU:32, one launch (start us, length us, event | category | flops | bytes accessed | tf_op | source)
XLA Modules:
  0.0 123.9 jit_solution(11512225479993328621)
XLA Ops:
  0.6 1.3 %reshape.27.vw = bf16[1,4608]{1,0:T(2,128)(2,1)} reshape(bf16[4608]{0:T(1024)(128)(2,1)} %param.14) | data formatting | bytes 18432 | tf_op jit(solution)/shard_map/reshape | solution.py:590
  1.9 114.2 %policy_head.1 = (bf16[640,4608]{1,0:T(8,128)(2,1)}, bf16[32,4608]{1,0:T(8,128)(2,1)}, f32[1,4608]{1,0:T(1,128)}) custom-call(bf16[32,4608]{1,0:T(8,128)(2,1)} %hs.1, bf16[640,4608]{1,0:T(8,128)(2,1)} %emb.1, s32[1,32]{1,0:T(1,128)} %bitcast.4, s32[1,32]{1,0:T(1,128)} %bitcast.5, bf16[1,32]{1,0:T(2,128)(2,1)} %bitcast.6, bf16[32,4608]{1,0:T(8,128)(2,1)} %cot.1, ...), custom_call_target="tpu_custom_call" | custom-call | tf_op jit(solution)/shard_map/policy_head/pallas_call | solution.py:540
  116.2 1.4 %reduce = f32[4608]{0:T(1024)} reduce(f32[1,4608]{1,0:T(1,128)} %get-tuple-element.8, f32[]{:T(128)} %constant.1), dimensions={0}, to_apply=%get-tuple-element.8.reduce_sub_computation | reduce | bytes 36868 | tf_op jit(solution)/shard_map/policy_head/pallas_call | solution.py:540
  117.5 0.0 copy-start
  117.5 5.7 %copy.13 = bf16[640,4608]{1,0:T(8,128)(2,1)} copy(bf16[640,4608]{1,0:T(8,128)(2,1)} %get-tuple-element.12) | data formatting | bytes 11796480
  123.2 0.0 copy-done
  123.2 0.7 copy.14
Async XLA Ops:
  117.5 5.7 %copy-start = (bf16[32,4608]{1,0:T(8,128)(2,1)S(1)}, bf16[32,4608]{1,0:T(8,128)(2,1)}, u32[]{:S(2)}) copy-start(bf16[32,4608]{1,0:T(8,128)(2,1)} %get-tuple-element.13) | copy-start | bytes 884740

commit v2 on v1

v2 whole, which is shorter than its diff:
```python
import math

import jax
import jax.numpy as jnp
from jax import lax
from jax.experimental import pallas as pl
from jax.experimental.pallas import tpu as pltpu
from jax.sharding import PartitionSpec as P

VALUE_SCALE = 0.5
MESH = pl.DeviceIdType.MESH
F32, BF16 = jnp.float32, jnp.bfloat16

ROWS = 32
TOK = 512
D = 4608
HALF = D // 2
PIECE = 768
QUART = PIECE // 2
VOC = 640
W = HALF // 2
SENDS = 224


def align(value, to=128):
    return pl.multiple_of(value, to)


def kernel(
    hs, emb, tid, tgt, coef, cot, vw, ret,
    ge, gh, gv,
    H, C, E, EH, LT, GS, GT, PA, PB, SA, SB, RA, RB, SA2, SB2, RA2, RB2,
    ZS, ZR, FZ, OUT, META, STA, RSA, STB, RSB, VB, VR, VW, LK,
    ss, rs, ls, xs,
):
    pipe, tensor = lax.axis_index("pipe"), lax.axis_index("tensor")
    x, zh = pipe // 4, pipe % 4
    zl, y, c = tensor // 8, (tensor // 2) % 4, tensor % 2
    z = 2 * zh + zl
    q = x % 2

    def dev(dx=0, dy=0, dz=0, dc=0):
        xx, yy, zz, cc = (x + dx) % 4, (y + dy) % 4, (z + dz + 8) % 8, (c + dc) % 2
        return xx * 4 + zz // 2, (zz % 2) * 8 + yy * 2 + cc

    pair = 1 - 2 * zl

    counter = [0]
    started = []

    def send(src, dst, target):
        k = counter[0]
        counter[0] += 1
        cp = pltpu.make_async_remote_copy(
            src_ref=src, dst_ref=dst, send_sem=ss.at[k], recv_sem=rs.at[k],
            device_id=target, device_id_type=MESH,
        )
        cp.start()
        started.append(cp)
        return cp

    def load(src, dst, k):
        cp = pltpu.make_async_copy(src, dst, ls.at[k])
        cp.start()
        return cp

    my_half = pl.ds(align(c * HALF), HALF)
    sib_half = pl.ds(align((1 - c) * HALF), HALF)
    ld_h = load(hs, H.at[0, 0, 0], 0)
    ld_e = load(emb, E, 1)
    ld_c = load(cot, C.at[0, 0, 0], 2)
    ld_eh = load(emb.at[:, my_half], EH.at[0:VOC], 3)

    plane = [(dx, dy) for dx in range(4) for dy in range(4) if (dx, dy) != (0, 0)]
    column = [(dz, dc) for dz in range(8) for dc in range(2) if (dz, dc) != (0, 0)]
    peers = [(dx, dy, 0, 0) for dx, dy in plane] + [(0, 0, dz, dc) for dz, dc in column]
    peers += [(dx, 0, 0, 1) for dx in (1, 2, 3)]
    bar = pltpu.get_barrier_semaphore()
    for peer in peers:
        pl.semaphore_signal(bar, inc=1, device_id=dev(*peer), device_id_type=MESH)

    META[0, 0, 0] = jnp.zeros((8, 128), F32)
    META[0, 0, 0, 0:1, 0:ROWS] = tid[...].astype(F32)
    META[0, 0, 0, 1:2, 0:ROWS] = tgt[...].astype(F32)
    META[0, 0, 0, 2:3, 0:ROWS] = coef[...].astype(F32)
    pl.semaphore_wait(bar, len(peers))

    def cols(half, j):
        return pl.ds(align(half * HALF + j * PIECE), PIECE)

    def quarter(half, j, k):
        return pl.ds(align(half * HALF + j * PIECE + k * QUART), QUART)

    class Gather:
        def __init__(self, X, by_z):
            self.X, self.by_z = X, by_z
            self.m = {}

        def again(self, key, part):
            pltpu.make_async_remote_copy(
                src_ref=part, dst_ref=part, send_sem=ss.at[self.m[key]], recv_sem=rs.at[self.m[key]],
                device_id=dev(dc=1), device_id_type=MESH,
            ).wait_recv()

        def begin(self):
            X, m = self.X, self.m
            order = sorted(range(3), key=lambda j: self.by_z[j])
            for j in order:
                if not self.by_z[j]:
                    self.zsend(j)
            for j in range(3):
                self.ysend(0, j)
                if j == 0:
                    m["s0"] = send(X.at[0, 0, 0], X.at[0, 0, 1], dev(dc=1))
            for j in order:
                if self.by_z[j]:
                    self.zsend(j)

        def zsend(self, j):
            X, m = self.X, self.m
            m["za", j] = send(X.at[0, 0, 0, :, cols(q, j)], X.at[0, 1, 0, :, cols(q, j)], dev(dz=1))
            m["zb", j] = send(X.at[0, 0, 0, :, cols(1 - q, j)], X.at[0, 1, 0, :, cols(1 - q, j)], dev(dz=-1))

        def ysend(self, dz, j):
            X, m = self.X, self.m
            for dy in (1, 3, 2):
                part = X.at[0, dz, 0, :, cols(q, j)]
                m["y", dz, dy, j] = send(part, X.at[dy, dz, 0, :, cols(q, j)], dev(dy=-dy))

        def s1(self, j):
            X, m = self.X, self.m
            m["za", j].wait_recv()
            if not self.by_z[j]:
                self.ysend(1, j)
            m["zb", j].wait_recv()
            for h, k in ((q, "sza"), (1 - q, "szb")):
                m[k, j] = send(X.at[0, 1, 0, :, cols(h, j)], X.at[0, 1, 1, :, cols(h, j)], dev(dc=1))

        def relay(self, dz, j):
            X, m = self.X, self.m
            for dy in (1, 2, 3):
                m["y", dz, dy, j].wait_recv()
            rows = pl.ds(1, 3)
            for k, dx in ((0, 1), (1, -1)):
                part = X.at[rows, dz, 0, :, quarter(q, j, k)]
                m["x", dz, k, j] = counter[0]
                send(part, part, dev(dx=dx))
            if self.by_z[j]:
                m["zc", j] = send(X.at[rows, 0, 0, :, cols(q, j)], X.at[rows, 1, 0, :, cols(q, j)], dev(dz=1))
            m["sy", dz, j] = send(
                X.at[rows, dz, 0, :, cols(q, j)], X.at[rows, dz, 1, :, cols(q, j)], dev(dc=1)
            )

        def s4(self, j):
            X, m = self.X, self.m
            rows = pl.ds(1, 3)
            for dz in range(1 if self.by_z[j] else 2):
                for k in range(2):
                    self.again(("x", dz, k, j), X.at[rows, dz, 0, :, quarter(1 - q, j, k)])
                part = cols(1 - q, j)
                if self.by_z[j]:
                    m["zd", j] = send(X.at[rows, 0, 0, :, part], X.at[rows, 1, 0, :, part], dev(dz=-1))
                m["sx", dz, j] = send(X.at[rows, dz, 0, :, part], X.at[rows, dz, 1, :, part], dev(dc=1))

        def s4z(self, j):
            X, m = self.X, self.m
            rows = pl.ds(1, 3)
            for key, back, h in (("zc", "sy", q), ("zd", "sx", 1 - q)):
                m[key, j].wait_recv()
                part = cols(h, j)
                m[back, 1, j] = send(X.at[rows, 1, 0, :, part], X.at[rows, 1, 1, :, part], dev(dc=1))

        def s5(self, j):
            m = self.m
            if j == 0:
                m["s0"].wait_recv()
            for k in ("sza", "szb"):
                m[k, j].wait_recv()
            for dz in range(2):
                m["sy", dz, j].wait_recv()
                m["sx", dz, j].wait_recv()

    gat_h, gat_c = Gather(H, (True, True, False)), Gather(C, (True, True, True))

    ld_h.wait()
    gat_h.begin()

    h_own = H[0, 0, 0].astype(F32)
    for k in range(D // 128):
        VW[:, k * 128 : (k + 1) * 128] = vw[k : k + 1, :].astype(F32)
    value_out = jnp.sum(h_own * VW[...], axis=1, keepdims=True)
    eye = lax.broadcasted_iota(jnp.int32, (ROWS, ROWS), 0) == lax.broadcasted_iota(jnp.int32, (ROWS, ROWS), 1)
    ret_col = jnp.sum(jnp.where(eye, jnp.broadcast_to(ret[...], (ROWS, ROWS)), 0.0), axis=1, keepdims=True)
    delta = VALUE_SCALE * (value_out - ret_col)
    META[0, 0, 0, 3:4, 0:ROWS] = jnp.sum(jnp.where(eye, delta, 0.0), axis=0, keepdims=True)
    VB[0] = jnp.sum(delta * h_own, axis=0, keepdims=True)
    me_s = send(META.at[0, 0, 0], META.at[0, 0, 1], dev(dc=1))
    vv = [send(VB.at[0], VR.at[0], dev(dc=1))]

    gat_h.s1(2)
    gat_h.relay(0, 0)
    ld_e.wait()
    eh_s = send(E.at[:, sib_half], EH.at[VOC : 2 * VOC], dev(dc=1))
    gat_h.s1(0)
    gat_h.relay(0, 1)
    gat_h.s1(1)
    gat_h.s4(0)
    gat_h.relay(0, 2)
    me_s.wait_recv()
    me_z = send(META.at[0, 0], META.at[0, 1], dev(dz=pair))
    gat_h.s4(1)
    gat_h.relay(1, 2)
    gat_h.s4z(0)
    me_z.wait_recv()
    me_y = [send(META.at[0], META.at[dy], dev(dy=-dy)) for dy in (1, 2, 3)]
    vv[0].wait_recv()

    def value_step(k, target):
        VB[k] = VB[k - 1] + VR[k - 1]
        vv.append(send(VB.at[k], VR.at[k], target))

    value_step(1, dev(dz=pair))
    gat_h.s5(0)

    def logits(j):
        def tile(n, _):
            total = jnp.zeros((VOC, 256), F32)
            for half in range(2):
                at = half * HALF + j * PIECE
                rows = H[pl.ds(2 * n, 2), :, :, :, at : at + PIECE].reshape(256, PIECE)
                total += lax.dot_general(
                    E[:, at : at + PIECE], rows, (((1,), (1,)), ((), ())), preferred_element_type=F32
                )
            where = (slice(None), pl.ds(align(n * 256, 256), 256))
            LT[where] = total if j == 0 else LT[where] + total
            return 0

        lax.fori_loop(0, 2, tile, 0)

    logits(0)
    gat_h.s4z(1)
    ld_c.wait()
    gat_c.begin()
    gat_h.s5(1)
    logits(1)
    gat_h.s4(2)
    vv[1].wait_recv()
    value_step(2, dev(dy=1 - 2 * (y % 2)))
    gat_h.s5(2)
    logits(2)

    peak = jnp.max(LT[...], axis=0, keepdims=True)
    total = jnp.sum(jnp.exp(LT[...] - peak), axis=0, keepdims=True)
    STA[0:1] = peak
    STA[1:2] = total
    sta = {}
    for dx, dy in plane:
        back = (-dx % 4) * 4 + (-dy % 4)
        sta[back] = send(STA, RSA.at[back], dev(dx=dx, dy=dy))

    def merge(stats):
        peaks = stats[0][0]
        for p, _ in stats[1:]:
            peaks = jnp.maximum(peaks, p)
        sums = sum(s * jnp.exp(p - peaks) for p, s in stats)
        return peaks, sums

    gat_c.s1(0)
    gat_c.relay(0, 0)

    stats = [(peak, total)]
    for dx, dy in plane:
        k = dx * 4 + dy
        sta[k].wait_recv()
        got = RSA[k]
        if dy:
            got = jnp.concatenate([got[:, 128 * (4 - dy) :], got[:, : 128 * (4 - dy)]], axis=1)
        stats.append((got[0:1], got[1:2]))
    peak, total = merge(stats)
    STB[0:1] = peak
    STB[1:2] = total
    stb = {}
    for dz, dc in column:
        back = (-dz % 8) * 2 + dc
        stb[back] = send(STB, RSB.at[back], dev(dz=dz, dc=dc))

    gat_c.s1(1)
    gat_c.relay(0, 1)
    gat_c.s4(0)

    lane = lax.broadcasted_iota(jnp.int32, (2, 128), 1)

    def reorder(p, s, odd, dc):
        both = jnp.concatenate([p, s], axis=0)
        groups = []
        for g in range(4):
            part = both[:, 128 * g : 128 * (g + 1)]
            if odd:
                part = pltpu.roll(part, 64, 1)
            if dc:
                part = jnp.where((lane // 32) % 2 == 0, pltpu.roll(part, 96, 1), pltpu.roll(part, 32, 1))
            groups.append(part)
        both = jnp.concatenate(groups, axis=1)
        return both[0:1], both[1:2]

    classes = []
    for odd in range(2):
        for dc in range(2):
            stats = []
            for dz in range(odd, 8, 2):
                k = dz * 2 + dc
                if k == 0:
                    stats.append((peak, total))
                    continue
                stb[k].wait_recv()
                got = RSB[k]
                stats.append((got[0:1], got[1:2]))
            classes.append(reorder(*merge(stats), odd, dc))
    peak, total = merge(classes)

    for cp in me_y:
        cp.wait_recv()

    def facts():
        groups = []
        for dy in range(4):
            part = META[dy, 0, 0]
            for k in range(1, 4):
                part = part + pltpu.roll(META[dy, k // 2, k % 2], 32 * k, 1)
            groups.append(part)
        return jnp.concatenate(groups, axis=1)

    fact = facts()
    offset = (pipe * 16 + tensor) * VOC
    coefs, target, token = fact[2:3], fact[1:2], fact[0:1]
    inverse = 1.0 / total

    for i in range(5):
        rows = pl.ds(i * 128, 128)
        vocab = (offset + i * 128 + lax.broadcasted_iota(jnp.int32, (128, 1), 0)).astype(F32)
        hit = (target == vocab).astype(F32)
        grad = coefs * (jnp.exp(LT[rows, :] - peak) * inverse - hit)
        GS[rows, :] = grad.astype(BF16)
        turned = grad.T.astype(BF16)
        GT[:, :, :, :, i * 128 : (i + 1) * 128] = turned.reshape(4, 2, 2, ROWS, 128)
    gts = [
        send(GT.at[:, :, k, :, 0:VOC], GT.at[:, :, 1 - k, :, VOC : 2 * VOC], dev(dc=1)) for k in range(2)
    ]
    gat_c.s1(2)
    gat_c.relay(0, 2)
    eh_s.wait_recv()
    ld_eh.wait()
    for cp in gts:
        cp.wait_recv()

    def block_of(dx):
        xx = (x + dx) % 4
        return (xx // 2 + zl) % 2, (xx % 2 + c) % 2

    dz0, dc0 = block_of(0)
    away = (x // 2 + zl) % 2
    tok_core = x % 2
    ra, rb, ra2, rb2, zk, gk, ok = {}, {}, {}, {}, {}, {}, {}

    def partial(k, base):
        at = pl.ds(base + k * QUART, QUART)
        return jnp.dot(
            GT[...].reshape(TOK, 2 * VOC), EH[:, at], preferred_element_type=F32
        ).reshape(4, 2, 2, ROWS, QUART)

    def r1(k):
        got = partial(k, 0)
        PA[k] = got[0]
        SA[k] = got.astype(BF16)
        ra[k] = [send(SA.at[k, dy], RA.at[k, dy - 1], dev(dy=dy)) for dy in (1, 3, 2)]
        got = partial(k, W)
        PB[k] = got
        SB[k] = got.astype(BF16)
        rb[k] = []
        for dx in (1, 3, 2):
            dz, dc = block_of(dx)
            rb[k].append(send(SB.at[k, :, dz, dc], RB.at[k, dx - 1], dev(dx=dx)))

    def r2(k):
        for cp in ra[k]:
            cp.wait_recv()
        total = PA[k]
        for i in range(3):
            total += RA[k, i].astype(F32)
        PA[k] = total
        SA2[k] = total.astype(BF16)
        ra2[k] = []
        for dx in (1, 3, 2):
            dz, dc = block_of(dx)
            ra2[k].append(send(SA2.at[k, dz, dc], RA2.at[k, dx - 1], dev(dx=dx)))
        for cp in rb[k]:
            cp.wait_recv()
        total = PB[k, :, dz0, dc0]
        for i in range(3):
            total += RB[k, i].astype(F32)
        PB[k, 0, 0, 0] = total[0]
        SB2[k] = total.astype(BF16)
        rb2[k] = [send(SB2.at[k, dy], RB2.at[k, dy - 1], dev(dy=dy)) for dy in (1, 3, 2)]

    def z_copy(k, i):
        zz = (z + away + 2 * i) % 8
        piece = zz // 2
        slot = away * 4 + i
        return pltpu.make_async_remote_copy(
            src_ref=ZS.at[k, piece // 2, piece % 2], dst_ref=ZR.at[k, slot], send_sem=ss.at[zk[k] + i],
            recv_sem=rs.at[zk[k] + slot], device_id=dev(dz=away + 2 * i), device_id_type=MESH,
        )

    def r3(k):
        for cp in ra2[k]:
            cp.wait_recv()
        total = PA[k, dz0, dc0]
        for i in range(3):
            total += RA2[k, i].astype(F32)
        ZS[k, 0] = total.astype(BF16).reshape(2, 16, QUART)
        for cp in rb2[k]:
            cp.wait_recv()
        total = PB[k, 0, 0, 0]
        for i in range(3):
            total += RB2[k, i].astype(F32)
        ZS[k, 1] = total.astype(BF16).reshape(2, 16, QUART)
        zk[k], gk[k], ok[k] = counter[0], counter[0] + 8, counter[0] + 11
        counter[0] += 15
        for i in range(1, 4):
            z_copy(k, i).start()

        @pl.when(away == 1)
        def _():
            z_copy(k, 0).start()

    def g_copy(k, i):
        part = FZ.at[k, zh // 2, zh % 2]
        return pltpu.make_async_remote_copy(
            src_ref=part, dst_ref=part, send_sem=ss.at[gk[k] + i - 1],
            recv_sem=rs.at[gk[k] + i - 1], device_id=dev(dz=2 * i), device_id_type=MESH,
        )

    def r4(k):
        @pl.when(away == 0)
        def _():
            for slot in range(1, 8):
                pltpu.make_async_remote_copy(
                    src_ref=ZR.at[k, slot], dst_ref=ZR.at[k, slot], send_sem=ss.at[zk[k]],
                    recv_sem=rs.at[zk[k] + slot], device_id=dev(dz=1), device_id_type=MESH,
                ).wait_recv()
            ab, rh = zh // 2, zh % 2
            acc = ZS[k, ab, rh].astype(F32)
            for slot in range(1, 8):
                acc += ZR[k, slot].astype(F32)
            row = META[0, 0, dc0, 3:4, :]
            lanes = lax.broadcasted_iota(jnp.int32, (16, 128), 1)
            picks = lanes == lax.broadcasted_iota(jnp.int32, (16, 128), 0) + 16 * rh
            delta16 = jnp.sum(jnp.where(picks, row, 0.0), axis=1, keepdims=True)
            wide = VW[:, pl.ds(align(c * HALF + ab * W + k * QUART), QUART)]
            FZ[k, ab, rh] = (acc + delta16 * wide).astype(BF16)
            for i in range(1, 4):
                g_copy(k, i).start()

    def o_copy(k, dx):
        xx = (x + dx) % 4
        return pltpu.make_async_remote_copy(
            src_ref=FZ.at[k], dst_ref=OUT.at[k, c], send_sem=ss.at[ok[k] + dx], recv_sem=rs.at[ok[k] + c],
            device_id=(xx * 4 + zh, zl * 8 + y * 2 + tok_core), device_id_type=MESH,
        )

    def r5(k):
        @pl.when(away == 0)
        def _():
            for i in range(1, 4):
                piece = (zh - i + 4) % 4
                part = FZ.at[k, piece // 2, piece % 2]
                pltpu.make_async_remote_copy(
                    src_ref=part, dst_ref=part, send_sem=ss.at[gk[k]], recv_sem=rs.at[gk[k] + i - 1],
                    device_id=dev(dz=2), device_id_type=MESH,
                ).wait_recv()
            for dx in (1, 3, 2):
                o_copy(k, dx).start()

            @pl.when(tok_core == c)
            def _():
                local = pltpu.make_async_copy(FZ.at[k], OUT.at[k, c], xs.at[k])
                local.start()
                local.wait()

            @pl.when(tok_core != c)
            def _():
                o_copy(k, 0).start()

    home = (zl * 2 + c) == x

    def r6(k):
        def o_wait(core):
            pltpu.make_async_remote_copy(
                src_ref=FZ.at[k], dst_ref=OUT.at[k, core], send_sem=ss.at[ok[k]], recv_sem=rs.at[ok[k] + core],
                device_id=dev(dx=1), device_id_type=MESH,
            ).wait_recv()

        o_wait(1 - c)

        @pl.when(jnp.logical_not(home))
        def _():
            o_wait(c)

        for cs in range(2):
            for ab in range(2):
                at = cs * HALF + ab * W + k * QUART
                for rh in range(2):
                    gh[rh * 16 : (rh + 1) * 16, at : at + QUART] = OUT[k, cs, ab, rh]

    vocab = (offset + lax.broadcasted_iota(jnp.int32, (VOC, 1), 0)).astype(F32)
    LK[...] = (token == vocab).astype(BF16)
    normalizer = math.sqrt(D)

    def embed(n):
        at = slice(n * PIECE, (n + 1) * PIECE)
        head = jnp.dot(GS[...], H[:, :, :, :, at].reshape(TOK, PIECE), preferred_element_type=F32)
        looked = jnp.dot(LK[...], C[:, :, :, :, at].reshape(TOK, PIECE), preferred_element_type=F32)
        ge[:, at] = (head + normalizer * looked).astype(BF16)

    r1(0)
    gat_c.s4(1)
    r1(1)
    gat_c.s4(2)
    r1(2)
    gat_c.s4z(0)
    vv[2].wait_recv()
    value_step(3, dev(dy=2))
    gat_c.s4z(1)
    gat_c.s5(0)
    embed(0)
    embed(3)
    r2(0)
    gat_c.s4z(2)
    gat_c.s5(1)
    embed(1)
    r2(1)
    r3(0)
    embed(4)
    gat_c.s5(2)
    r2(2)
    r3(1)
    r4(0)
    embed(2)
    r3(2)
    r4(1)
    r5(0)
    embed(5)
    r4(2)
    r5(1)
    r5(2)

    vv[3].wait_recv()
    for k in range(D // 128):
        at = slice(k * 128, (k + 1) * 128)
        gv[k : k + 1, :] = VB[3, :, at] + VR[3, :, at]

    for k in range(3):
        r6(k)

    assert counter[0] <= SENDS, counter[0]
    for cp in started:
        cp.wait_send()
    for k in range(3):
        for i in range(1, 4):
            z_copy(k, i).wait_send()

    @pl.when(away == 1)
    def _():
        for k in range(3):
            z_copy(k, 0).wait_send()

    @pl.when(away == 0)
    def _():
        for k in range(3):
            for i in range(1, 4):
                g_copy(k, i).wait_send()
            for dx in (1, 3, 2):
                o_copy(k, dx).wait_send()

        @pl.when(tok_core != c)
        def _():
            for k in range(3):
                o_copy(k, 0).wait_send()


def local(hidden_states, embedding, token_ids, target_ids, coefficients, cotangent, value_weight, returns):
    vmem, anywhere = pl.BlockSpec(memory_space=pltpu.VMEM), pl.BlockSpec(memory_space=pl.ANY)
    V, dma = pltpu.VMEM, pltpu.SemaphoreType.DMA
    ge, gh, gv = pl.pallas_call(
        kernel,
        out_shape=(
            pltpu.VMEM((VOC, D), BF16),
            pltpu.VMEM((ROWS, D), BF16),
            pltpu.VMEM((D // 128, 128), F32),
        ),
        in_specs=[anywhere, anywhere, vmem, vmem, vmem, anywhere, vmem, vmem],
        out_specs=(vmem, vmem, vmem),
        scratch_shapes=[
            V((4, 2, 2, ROWS, D), BF16),
            V((4, 2, 2, ROWS, D), BF16),
            V((VOC, D), BF16),
            V((2 * VOC, HALF), BF16),
            V((VOC, TOK), F32),
            V((VOC, TOK), BF16),
            V((4, 2, 2, ROWS, 2 * VOC), BF16),
            V((3, 2, 2, ROWS, QUART), F32),
            V((3, 4, 2, 2, ROWS, QUART), F32),
            V((3, 4, 2, 2, ROWS, QUART), BF16),
            V((3, 4, 2, 2, ROWS, QUART), BF16),
            V((3, 3, 2, 2, ROWS, QUART), BF16),
            V((3, 3, 4, ROWS, QUART), BF16),
            V((3, 2, 2, ROWS, QUART), BF16),
            V((3, 4, ROWS, QUART), BF16),
            V((3, 3, ROWS, QUART), BF16),
            V((3, 3, ROWS, QUART), BF16),
            V((3, 2, 2, 16, QUART), BF16),
            V((3, 8, 16, QUART), BF16),
            V((3, 2, 2, 16, QUART), BF16),
            V((3, 2, 2, 2, 16, QUART), BF16),
            V((4, 2, 2, 8, 128), F32),
            V((2, TOK), F32),
            V((16, 2, TOK), F32),
            V((2, TOK), F32),
            V((16, 2, TOK), F32),
            V((4, 1, D), F32),
            V((4, 1, D), F32),
            V((1, D), F32),
            V((VOC, TOK), BF16),
            dma((SENDS,)),
            dma((SENDS,)),
            dma((10,)),
            dma((3,)),
        ],
        compiler_params=pltpu.CompilerParams(
            collective_id=0, has_side_effects=True, vmem_limit_bytes=50 << 20
        ),
        name="policy_head",
    )(
        hidden_states, embedding, token_ids.reshape(1, ROWS), target_ids.reshape(1, ROWS),
        coefficients.reshape(1, ROWS), cotangent, value_weight.reshape(D // 128, 128), returns.reshape(1, ROWS),
    )
    return ge, gh, gv.reshape(D)


def solution(mesh):
    in_specs = (
        P("tensor", None),
        P(("pipe", "tensor"), None),
        P("tensor"),
        P("tensor"),
        P("tensor"),
        P("tensor", None),
        P(),
        P("tensor"),
    )
    out_specs = (P(("pipe", "tensor"), None), P("tensor", None), P())
    return jax.shard_map(local, mesh=mesh, in_specs=in_specs, out_specs=out_specs, check_vma=False)
```

time: 124 us -> 92.9 us (0.75)
  Pallas kernels: 114 us -> 88.2 us
  local copies, waits for them, and re-layouts: 7.71 us -> 3.9 us
  other arithmetic: 1.38 us -> 0 us
    pallas_call x1, Pallas kernels: 114 us -> 88.2 us  [local(): pl.pallas_call(kernel, out_shape=(pltpu.VMEM((VOC, D), BF16), pltpu.VMEM(...]
    unnamed x4 -> x3, local copies, waits for them, and re-layouts: 6.39 us -> 3.9 us
    pallas_call x1 -> x0, other arithmetic: 1.38 us -> none  [local(): pl.pallas_call(kernel, out_shape=(jax.ShapeDtypeStruct((VOC, D), BF16), j...]
    reshape x1 -> x0, local copies, waits for them, and re-layouts: 1.32 us -> none  [local(): value_weight.reshape(1, D)]
where the time goes in v2:
time: 92.9 us; the launch traced here: 92.7 us
  Pallas kernels  88.2 us (95%)
  local copies, waits for them, and re-layouts  3.9 us (4%)
    pallas_call x1, Pallas kernels, local(): pl.pallas_call(kernel, out_shape=(pltpu.VMEM((VOC, D), BF16), pltpu.VMEM(...  88.2 us
    unnamed x3, local copies, waits for them, and re-layouts  3.9 us

profile of v2, /device:TPU:32, one launch (start us, length us, event | category | flops | bytes accessed | tf_op | source)
XLA Modules:
  0.0 92.7 jit_solution(10904978884115549376)
XLA Ops:
  0.6 88.2 %policy_head.1 = (bf16[640,4608]{1,0:T(8,128)(2,1)S(1)}, bf16[32,4608]{1,0:T(8,128)(2,1)S(1)}, f32[36,128]{1,0:T(8,128)S(1)}) custom-call(bf16[32,4608]{1,0:T(8,128)(2,1)} %hs.1, bf16[640,4608]{1,0:T(8,128)(2,1)} %emb.1, s32[1,32]{1,0:T(1,128)} %bitcast.8, s32[1,32]{1,0:T(1,128)} %bitcast.9, bf16[1,32]{1,0:T(2,128)(2,1)} %bitcast.10, bf16[32,4608]{1,0:T(8,128)(2,1)} %cot.1, ...), custom_call_target="tpu_custom_call" | custom-call | tf_op jit(solution)/shard_map/policy_head/pallas_call | solution.py:594
  88.8 2.6 %copy.14 = bf16[640,4608]{1,0:T(8,128)(2,1)} copy(bf16[640,4608]{1,0:T(8,128)(2,1)S(1)} %get-tuple-element.9) | data formatting | bytes 11796480
  91.4 0.6 copy.16
  92.0 0.7 copy.15

commit v3 on v2

--- a/solution.py
+++ b/solution.py
@@ -19,7 +19,7 @@
 QUART = PIECE // 2
 VOC = 640
 W = HALF // 2
-SENDS = 224
+SENDS = 256
 
 
 def align(value, to=128):
@@ -31,7 +31,7 @@
     ge, gh, gv,
     H, C, E, EH, LT, GS, GT, PA, PB, SA, SB, RA, RB, SA2, SB2, RA2, RB2,
     ZS, ZR, FZ, OUT, META, STA, RSA, STB, RSB, VB, VR, VW, LK,
-    ss, rs, ls, xs,
+    ss, rs, ls,
 ):
     pipe, tensor = lax.axis_index("pipe"), lax.axis_index("tensor")
     x, zh = pipe // 4, pipe % 4
@@ -59,6 +59,17 @@
         started.append(cp)
         return cp
 
+    gone = set()
+
+    def left(cp):
+        if id(cp) not in gone:
+            gone.add(id(cp))
+            cp.wait_send()
+
+    def flush(first=None):
+        for cp in started[:first]:
+            left(cp)
+
     def load(src, dst, k):
         cp = pltpu.make_async_copy(src, dst, ls.at[k])
         cp.start()
@@ -73,8 +84,8 @@
 
     plane = [(dx, dy) for dx in range(4) for dy in range(4) if (dx, dy) != (0, 0)]
     column = [(dz, dc) for dz in range(8) for dc in range(2) if (dz, dc) != (0, 0)]
-    peers = [(dx, dy, 0, 0) for dx, dy in plane] + [(0, 0, dz, dc) for dz, dc in column]
-    peers += [(dx, 0, 0, 1) for dx in (1, 2, 3)]
+    peers = [(d, 0, 0, 0) for d in (1, 2, 3)] + [(0, d, 0, 0) for d in (1, 2, 3)]
+    peers += [(0, 0, d, 0) for d in range(1, 8)] + [(0, 0, 0, 1)]
     bar = pltpu.get_barrier_semaphore()
     for peer in peers:
         pl.semaphore_signal(bar, inc=1, device_id=dev(*peer), device_id_type=MESH)
@@ -102,19 +113,13 @@
                 device_id=dev(dc=1), device_id_type=MESH,
             ).wait_recv()
 
-        def begin(self):
-            X, m = self.X, self.m
-            order = sorted(range(3), key=lambda j: self.by_z[j])
-            for j in order:
-                if not self.by_z[j]:
-                    self.zsend(j)
-            for j in range(3):
-                self.ysend(0, j)
-                if j == 0:
-                    m["s0"] = send(X.at[0, 0, 0], X.at[0, 0, 1], dev(dc=1))
-            for j in order:
-                if self.by_z[j]:
-                    self.zsend(j)
+        def own(self):
+            self.m["s0"] = send(self.X.at[0, 0, 0], self.X.at[0, 0, 1], dev(dc=1))
+
+        def gate(self, j):
+            for dz in range(1 if self.by_z[j] else 2):
+                for dy in (1, 3, 2):
+                    left(self.m["y", dz, dy, j])
 
         def zsend(self, j):
             X, m = self.X, self.m
@@ -127,11 +132,14 @@
                 part = X.at[0, dz, 0, :, cols(q, j)]
                 m["y", dz, dy, j] = send(part, X.at[dy, dz, 0, :, cols(q, j)], dev(dy=-dy))
 
+        def s0(self, j):
+            self.m["za", j].wait_recv()
+            self.ysend(1, j)
+
         def s1(self, j):
             X, m = self.X, self.m
-            m["za", j].wait_recv()
-            if not self.by_z[j]:
-                self.ysend(1, j)
+            if self.by_z[j]:
+                m["za", j].wait_recv()
             m["zb", j].wait_recv()
             for h, k in ((q, "sza"), (1 - q, "szb")):
                 m[k, j] = send(X.at[0, 1, 0, :, cols(h, j)], X.at[0, 1, 1, :, cols(h, j)], dev(dc=1))
@@ -180,10 +188,15 @@
                 m["sy", dz, j].wait_recv()
                 m["sx", dz, j].wait_recv()
 
-    gat_h, gat_c = Gather(H, (True, True, False)), Gather(C, (True, True, True))
+    gat_h, gat_c = Gather(H, (True, False, False)), Gather(C, (True, True, True))
 
     ld_h.wait()
-    gat_h.begin()
+    gat_h.zsend(1)
+    gat_h.ysend(0, 0)
+    gat_h.zsend(2)
+    gat_h.zsend(0)
+    gat_h.own()
+    eh_s = send(emb.at[:, sib_half], EH.at[VOC : 2 * VOC], dev(dc=1))
 
     h_own = H[0, 0, 0].astype(F32)
     for k in range(D // 128):
@@ -197,19 +210,26 @@
     me_s = send(META.at[0, 0, 0], META.at[0, 0, 1], dev(dc=1))
     vv = [send(VB.at[0], VR.at[0], dev(dc=1))]
 
+    gat_h.gate(0)
+    gat_h.ysend(0, 1)
+    gat_h.s0(1)
+    gat_h.relay(0, 0)
+    gat_h.s1(1)
+    gat_h.gate(1)
+    gat_h.ysend(0, 2)
+    gat_h.s0(2)
+    gat_h.relay(0, 1)
+    gat_h.relay(1, 1)
+    gat_h.s4(0)
+    gat_h.s1(0)
     gat_h.s1(2)
-    gat_h.relay(0, 0)
-    ld_e.wait()
-    eh_s = send(E.at[:, sib_half], EH.at[VOC : 2 * VOC], dev(dc=1))
-    gat_h.s1(0)
-    gat_h.relay(0, 1)
-    gat_h.s1(1)
-    gat_h.s4(0)
-    gat_h.relay(0, 2)
     me_s.wait_recv()
     me_z = send(META.at[0, 0], META.at[0, 1], dev(dz=pair))
+    gat_h.relay(0, 2)
     gat_h.s4(1)
     gat_h.relay(1, 2)
+    ld_c.wait()
+    gat_c.ysend(0, 0)
     gat_h.s4z(0)
     me_z.wait_recv()
     me_y = [send(META.at[0], META.at[dy], dev(dy=-dy)) for dy in (1, 2, 3)]
@@ -237,15 +257,16 @@
 
         lax.fori_loop(0, 2, tile, 0)
 
+    ld_e.wait()
     logits(0)
-    gat_h.s4z(1)
-    ld_c.wait()
-    gat_c.begin()
     gat_h.s5(1)
     logits(1)
     gat_h.s4(2)
     vv[1].wait_recv()
     value_step(2, dev(dy=1 - 2 * (y % 2)))
+    gat_c.gate(0)
+    gat_c.ysend(0, 1)
+    gat_c.zsend(0)
     gat_h.s5(2)
     logits(2)
 
@@ -253,6 +274,7 @@
     total = jnp.sum(jnp.exp(LT[...] - peak), axis=0, keepdims=True)
     STA[0:1] = peak
     STA[1:2] = total
+    before_stats = len(started)
     sta = {}
     for dx, dy in plane:
         back = (-dx % 4) * 4 + (-dy % 4)
@@ -265,8 +287,10 @@
         sums = sum(s * jnp.exp(p - peaks) for p, s in stats)
         return peaks, sums
 
-    gat_c.s1(0)
+    flush(before_stats)
+    gat_c.ysend(0, 2)
     gat_c.relay(0, 0)
+    gat_c.own()
 
     stats = [(peak, total)]
     for dx, dy in plane:
@@ -284,8 +308,10 @@
         back = (-dz % 8) * 2 + dc
         stb[back] = send(STB, RSB.at[back], dev(dz=dz, dc=dc))
 
-    gat_c.s1(1)
+    gat_c.s1(0)
     gat_c.relay(0, 1)
+    gat_c.zsend(1)
+    gat_c.zsend(2)
     gat_c.s4(0)
 
     lane = lax.broadcasted_iota(jnp.int32, (2, 128), 1)
@@ -346,6 +372,7 @@
     gts = [
         send(GT.at[:, :, k, :, 0:VOC], GT.at[:, :, 1 - k, :, VOC : 2 * VOC], dev(dc=1)) for k in range(2)
     ]
+    gat_c.s1(1)
     gat_c.s1(2)
     gat_c.relay(0, 2)
     eh_s.wait_recv()
@@ -360,7 +387,8 @@
     dz0, dc0 = block_of(0)
     away = (x // 2 + zl) % 2
     tok_core = x % 2
-    ra, rb, ra2, rb2, zk, gk, ok = {}, {}, {}, {}, {}, {}, {}
+    ra, rb, ra2, rb2, zk, gk = {}, {}, {}, {}, {}, {}
+    others = [(dx, i) for dx in (1, 3, 2, 0) for i in (1, 3, 2, 0) if (dx, i) != (0, 0)]
 
     def partial(k, base):
         at = pl.ds(base + k * QUART, QUART)
@@ -368,14 +396,22 @@
             GT[...].reshape(TOK, 2 * VOC), EH[:, at], preferred_element_type=F32
         ).reshape(4, 2, 2, ROWS, QUART)
 
-    def r1(k):
+    def p1(k):
         got = partial(k, 0)
         PA[k] = got[0]
         SA[k] = got.astype(BF16)
-        ra[k] = [send(SA.at[k, dy], RA.at[k, dy - 1], dev(dy=dy)) for dy in (1, 3, 2)]
         got = partial(k, W)
         PB[k] = got
         SB[k] = got.astype(BF16)
+
+    def r1(k):
+        if k:
+            for cp in ra[k - 1]:
+                left(cp)
+        ra[k] = [send(SA.at[k, dy], RA.at[k, dy - 1], dev(dy=dy)) for dy in (1, 3, 2)]
+        if k:
+            for cp in rb[k - 1]:
+                left(cp)
         rb[k] = []
         for dx in (1, 3, 2):
             dz, dc = block_of(dx)
@@ -424,8 +460,8 @@
         for i in range(3):
             total += RB2[k, i].astype(F32)
         ZS[k, 1] = total.astype(BF16).reshape(2, 16, QUART)
-        zk[k], gk[k], ok[k] = counter[0], counter[0] + 8, counter[0] + 11
-        counter[0] += 15
+        zk[k], gk[k] = counter[0], counter[0] + 8
+        counter[0] += 24
         for i in range(1, 4):
             z_copy(k, i).start()
 
@@ -433,11 +469,11 @@
         def _():
             z_copy(k, 0).start()
 
-    def g_copy(k, i):
-        part = FZ.at[k, zh // 2, zh % 2]
+    def o_copy(k, dx, i):
+        part = FZ.at[k]
         return pltpu.make_async_remote_copy(
-            src_ref=part, dst_ref=part, send_sem=ss.at[gk[k] + i - 1],
-            recv_sem=rs.at[gk[k] + i - 1], device_id=dev(dz=2 * i), device_id_type=MESH,
+            src_ref=part, dst_ref=OUT.at[k, c, zh // 2, zh % 2], send_sem=ss.at[gk[k] + dx * 4 + i],
+            recv_sem=rs.at[gk[k] + c * 4 + zh], device_id=dev(dx, 0, 2 * i, tok_core + c), device_id_type=MESH,
         )
 
     def r4(k):
@@ -457,54 +493,35 @@
             picks = lanes == lax.broadcasted_iota(jnp.int32, (16, 128), 0) + 16 * rh
             delta16 = jnp.sum(jnp.where(picks, row, 0.0), axis=1, keepdims=True)
             wide = VW[:, pl.ds(align(c * HALF + ab * W + k * QUART), QUART)]
-            FZ[k, ab, rh] = (acc + delta16 * wide).astype(BF16)
-            for i in range(1, 4):
-                g_copy(k, i).start()
-
-    def o_copy(k, dx):
-        xx = (x + dx) % 4
-        return pltpu.make_async_remote_copy(
-            src_ref=FZ.at[k], dst_ref=OUT.at[k, c], send_sem=ss.at[ok[k] + dx], recv_sem=rs.at[ok[k] + c],
-            device_id=(xx * 4 + zh, zl * 8 + y * 2 + tok_core), device_id_type=MESH,
-        )
-
-    def r5(k):
-        @pl.when(away == 0)
-        def _():
-            for i in range(1, 4):
-                piece = (zh - i + 4) % 4
-                part = FZ.at[k, piece // 2, piece % 2]
-                pltpu.make_async_remote_copy(
-                    src_ref=part, dst_ref=part, send_sem=ss.at[gk[k]], recv_sem=rs.at[gk[k] + i - 1],
-                    device_id=dev(dz=2), device_id_type=MESH,
-                ).wait_recv()
-            for dx in (1, 3, 2):
-                o_copy(k, dx).start()
+            FZ[k] = (acc + delta16 * wide).astype(BF16)
+            for dx, i in others:
+                o_copy(k, dx, i).start()
 
             @pl.when(tok_core == c)
             def _():
-                local = pltpu.make_async_copy(FZ.at[k], OUT.at[k, c], xs.at[k])
-                local.start()
-                local.wait()
+                OUT[k, c, ab, rh] = FZ[k]
 
             @pl.when(tok_core != c)
             def _():
-                o_copy(k, 0).start()
+                o_copy(k, 0, 0).start()
 
     home = (zl * 2 + c) == x
 
     def r6(k):
-        def o_wait(core):
+        def o_wait(core, piece):
             pltpu.make_async_remote_copy(
-                src_ref=FZ.at[k], dst_ref=OUT.at[k, core], send_sem=ss.at[ok[k]], recv_sem=rs.at[ok[k] + core],
-                device_id=dev(dx=1), device_id_type=MESH,
+                src_ref=FZ.at[k], dst_ref=OUT.at[k, core, piece // 2, piece % 2], send_sem=ss.at[gk[k]],
+                recv_sem=rs.at[gk[k] + core * 4 + piece], device_id=dev(dx=1), device_id_type=MESH,
             ).wait_recv()
 
-        o_wait(1 - c)
+        for i in range(4):
+            o_wait(1 - c, i)
+        for i in range(1, 4):
+            o_wait(c, (zh + i) % 4)
 
         @pl.when(jnp.logical_not(home))
         def _():
-            o_wait(c)
+            o_wait(c, zh)
 
         for cs in range(2):
             for ab in range(2):
@@ -522,37 +539,38 @@
         looked = jnp.dot(LK[...], C[:, :, :, :, at].reshape(TOK, PIECE), preferred_element_type=F32)
         ge[:, at] = (head + normalizer * looked).astype(BF16)
 
+    p1(0)
     r1(0)
+    p1(1)
     gat_c.s4(1)
     r1(1)
+    p1(2)
     gat_c.s4(2)
-    r1(2)
     gat_c.s4z(0)
     vv[2].wait_recv()
     value_step(3, dev(dy=2))
+    r2(0)
+    r1(2)
     gat_c.s4z(1)
     gat_c.s5(0)
     embed(0)
     embed(3)
-    r2(0)
+    r2(1)
+    r3(0)
     gat_c.s4z(2)
     gat_c.s5(1)
     embed(1)
-    r2(1)
-    r3(0)
-    embed(4)
-    gat_c.s5(2)
     r2(2)
     r3(1)
     r4(0)
-    embed(2)
+    embed(4)
+    gat_c.s5(2)
+    flush()
     r3(2)
     r4(1)
-    r5(0)
+    embed(2)
+    r4(2)
     embed(5)
-    r4(2)
-    r5(1)
-    r5(2)
 
     vv[3].wait_recv()
     for k in range(D // 128):
@@ -563,8 +581,7 @@
         r6(k)
 
     assert counter[0] <= SENDS, counter[0]
-    for cp in started:
-        cp.wait_send()
+    flush()
     for k in range(3):
         for i in range(1, 4):
             z_copy(k, i).wait_send()
@@ -577,15 +594,13 @@
     @pl.when(away == 0)
     def _():
         for k in range(3):
-            for i in range(1, 4):
-                g_copy(k, i).wait_send()
-            for dx in (1, 3, 2):
-                o_copy(k, dx).wait_send()
+            for dx, i in others:
+                o_copy(k, dx, i).wait_send()
 
         @pl.when(tok_core != c)
         def _():
             for k in range(3):
-                o_copy(k, 0).wait_send()
+                o_copy(k, 0, 0).wait_send()
 
 
 def local(hidden_states, embedding, token_ids, target_ids, coefficients, cotangent, value_weight, returns):
@@ -620,7 +635,7 @@
             V((3, 3, ROWS, QUART), BF16),
             V((3, 2, 2, 16, QUART), BF16),
             V((3, 8, 16, QUART), BF16),
-            V((3, 2, 2, 16, QUART), BF16),
+            V((3, 16, QUART), BF16),
             V((3, 2, 2, 2, 16, QUART), BF16),
             V((4, 2, 2, 8, 128), F32),
             V((2, TOK), F32),
@@ -634,7 +649,6 @@
             dma((SENDS,)),
             dma((SENDS,)),
             dma((10,)),
-            dma((3,)),
         ],
         compiler_params=pltpu.CompilerParams(
             collective_id=0, has_side_effects=True, vmem_limit_bytes=50 << 20

time: 92.9 us -> 92.5 us (level)
  no operation moved by 1% of the time
where the time goes in v3:
time: 92.5 us; the launch traced here: 92.4 us
  Pallas kernels  87.9 us (95%)
  local copies, waits for them, and re-layouts  3.9 us (4%)
    pallas_call x1, Pallas kernels, local(): pl.pallas_call(kernel, out_shape=(pltpu.VMEM((VOC, D), BF16), pltpu.VMEM(...  87.9 us
    unnamed x3, local copies, waits for them, and re-layouts  3.9 us

profile of v3, /device:TPU:32, one launch (start us, length us, event | category | flops | bytes accessed | tf_op | source)
XLA Modules:
  0.0 92.4 jit_solution(10528922663644094532)
XLA Ops:
  0.6 87.9 %policy_head.1 = (bf16[640,4608]{1,0:T(8,128)(2,1)S(1)}, bf16[32,4608]{1,0:T(8,128)(2,1)S(1)}, f32[36,128]{1,0:T(8,128)S(1)}) custom-call(bf16[32,4608]{1,0:T(8,128)(2,1)} %hs.1, bf16[640,4608]{1,0:T(8,128)(2,1)} %emb.1, s32[1,32]{1,0:T(1,128)} %bitcast.8, s32[1,32]{1,0:T(1,128)} %bitcast.9, bf16[1,32]{1,0:T(2,128)(2,1)} %bitcast.10, bf16[32,4608]{1,0:T(8,128)(2,1)} %cot.1, ...), custom_call_target="tpu_custom_call" | custom-call | tf_op jit(solution)/shard_map/policy_head/pallas_call | solution.py:609
  88.5 2.6 %copy.14 = bf16[640,4608]{1,0:T(8,128)(2,1)} copy(bf16[640,4608]{1,0:T(8,128)(2,1)S(1)} %get-tuple-element.9) | data formatting | bytes 11796480
  91.1 0.6 copy.16
  91.7 0.7 copy.15

commit v4 on v3

--- a/solution.py
+++ b/solution.py
@@ -20,6 +20,8 @@
 VOC = 640
 W = HALF // 2
 SENDS = 256
+WIDE = 512
+PARTS = ((0, 512), (512, 384), (896, 256))
 
 
 def align(value, to=128):
@@ -84,6 +86,8 @@
 
     plane = [(dx, dy) for dx in range(4) for dy in range(4) if (dx, dy) != (0, 0)]
     column = [(dz, dc) for dz in range(8) for dc in range(2) if (dz, dc) != (0, 0)]
+    plane.sort(key=lambda d: -min(d[0], 4 - d[0]) - min(d[1], 4 - d[1]))
+    column.sort(key=lambda d: -min(d[0], 8 - d[0]))
     peers = [(d, 0, 0, 0) for d in (1, 2, 3)] + [(0, d, 0, 0) for d in (1, 2, 3)]
     peers += [(0, 0, d, 0) for d in range(1, 8)] + [(0, 0, 0, 1)]
     bar = pltpu.get_barrier_semaphore()
@@ -271,7 +275,10 @@
     logits(2)
 
     peak = jnp.max(LT[...], axis=0, keepdims=True)
-    total = jnp.sum(jnp.exp(LT[...] - peak), axis=0, keepdims=True)
+    weights = jnp.exp(LT[...] - peak)
+    LT[...] = weights
+    total = jnp.sum(weights, axis=0, keepdims=True)
+    own_peak = peak
     STA[0:1] = peak
     STA[1:2] = total
     before_stats = len(started)
@@ -293,7 +300,7 @@
     gat_c.own()
 
     stats = [(peak, total)]
-    for dx, dy in plane:
+    for dx, dy in reversed(plane):
         k = dx * 4 + dy
         sta[k].wait_recv()
         got = RSA[k]
@@ -359,19 +366,21 @@
     fact = facts()
     offset = (pipe * 16 + tensor) * VOC
     coefs, target, token = fact[2:3], fact[1:2], fact[0:1]
-    inverse = 1.0 / total
-
+    factor = jnp.exp(own_peak - peak) / total
+    gts = []
     for i in range(5):
         rows = pl.ds(i * 128, 128)
         vocab = (offset + i * 128 + lax.broadcasted_iota(jnp.int32, (128, 1), 0)).astype(F32)
         hit = (target == vocab).astype(F32)
-        grad = coefs * (jnp.exp(LT[rows, :] - peak) * inverse - hit)
-        GS[rows, :] = grad.astype(BF16)
-        turned = grad.T.astype(BF16)
+        grad = (coefs * (LT[rows, :] * factor - hit)).astype(BF16)
+        GS[rows, :] = grad
+        turned = grad.T
         GT[:, :, :, :, i * 128 : (i + 1) * 128] = turned.reshape(4, 2, 2, ROWS, 128)
-    gts = [
-        send(GT.at[:, :, k, :, 0:VOC], GT.at[:, :, 1 - k, :, VOC : 2 * VOC], dev(dc=1)) for k in range(2)
-    ]
+        if i in (2, 4):
+            done = (0, 384) if i == 2 else (384, 256)
+            for k in range(2):
+                here, there = pl.ds(*done), pl.ds(VOC + done[0], done[1])
+                gts.append(send(GT.at[:, :, k, :, here], GT.at[:, :, 1 - k, :, there], dev(dc=1)))
     gat_c.s1(1)
     gat_c.s1(2)
     gat_c.relay(0, 2)
@@ -388,78 +397,85 @@
     away = (x // 2 + zl) % 2
     tok_core = x % 2
     ra, rb, ra2, rb2, zk, gk = {}, {}, {}, {}, {}, {}
-    others = [(dx, i) for dx in (1, 3, 2, 0) for i in (1, 3, 2, 0) if (dx, i) != (0, 0)]
+    others = [(dx, i) for dx in (2, 1, 3, 0) for i in (2, 1, 3, 0) if (dx, i) != (0, 0)]
 
     def partial(k, base):
-        at = pl.ds(base + k * QUART, QUART)
+        first, wide = PARTS[k]
+        at = slice(base + first, base + first + wide)
         return jnp.dot(
             GT[...].reshape(TOK, 2 * VOC), EH[:, at], preferred_element_type=F32
-        ).reshape(4, 2, 2, ROWS, QUART)
-
-    def p1(k):
+        ).reshape(4, 2, 2, ROWS, wide)
+
+    def p1a(k):
         got = partial(k, 0)
-        PA[k] = got[0]
-        SA[k] = got.astype(BF16)
+        PA[k, :, :, :, : got.shape[-1]] = got[0]
+        SA[k, ..., : got.shape[-1]] = got.astype(BF16)
+
+    def p1b(k):
         got = partial(k, W)
-        PB[k] = got
-        SB[k] = got.astype(BF16)
-
-    def r1(k):
-        if k:
-            for cp in ra[k - 1]:
-                left(cp)
-        ra[k] = [send(SA.at[k, dy], RA.at[k, dy - 1], dev(dy=dy)) for dy in (1, 3, 2)]
-        if k:
-            for cp in rb[k - 1]:
-                left(cp)
+        PB[k, ..., : got.shape[-1]] = got
+        SB[k, ..., : got.shape[-1]] = got.astype(BF16)
+
+    def r1a(k):
+        wide = pl.ds(0, PARTS[k][1])
+        ra[k] = [
+            send(SA.at[k, dy, :, :, :, wide], RA.at[k, dy - 1, :, :, :, wide], dev(dy=dy)) for dy in (1, 3, 2)
+        ]
+
+    def r1b(k):
+        wide = pl.ds(0, PARTS[k][1])
         rb[k] = []
         for dx in (1, 3, 2):
             dz, dc = block_of(dx)
-            rb[k].append(send(SB.at[k, :, dz, dc], RB.at[k, dx - 1], dev(dx=dx)))
+            rb[k].append(send(SB.at[k, :, dz, dc, :, wide], RB.at[k, dx - 1, :, :, wide], dev(dx=dx)))
 
     def r2(k):
+        wide = pl.ds(0, PARTS[k][1])
         for cp in ra[k]:
             cp.wait_recv()
-        total = PA[k]
+        total = PA[k, :, :, :, wide]
         for i in range(3):
-            total += RA[k, i].astype(F32)
-        PA[k] = total
-        SA2[k] = total.astype(BF16)
+            total += RA[k, i, :, :, :, wide].astype(F32)
+        PA[k, :, :, :, wide] = total
+        SA2[k, :, :, :, wide] = total.astype(BF16)
         ra2[k] = []
         for dx in (1, 3, 2):
             dz, dc = block_of(dx)
-            ra2[k].append(send(SA2.at[k, dz, dc], RA2.at[k, dx - 1], dev(dx=dx)))
+            ra2[k].append(send(SA2.at[k, dz, dc, :, wide], RA2.at[k, dx - 1, :, wide], dev(dx=dx)))
         for cp in rb[k]:
             cp.wait_recv()
-        total = PB[k, :, dz0, dc0]
+        total = PB[k, :, dz0, dc0, :, wide]
         for i in range(3):
-            total += RB[k, i].astype(F32)
-        PB[k, 0, 0, 0] = total[0]
-        SB2[k] = total.astype(BF16)
-        rb2[k] = [send(SB2.at[k, dy], RB2.at[k, dy - 1], dev(dy=dy)) for dy in (1, 3, 2)]
+            total += RB[k, i, :, :, wide].astype(F32)
+        PB[k, 0, 0, 0, :, wide] = total[0]
+        SB2[k, :, :, wide] = total.astype(BF16)
+        rb2[k] = [send(SB2.at[k, dy, :, wide], RB2.at[k, dy - 1, :, wide], dev(dy=dy)) for dy in (1, 3, 2)]
 
     def z_copy(k, i):
         zz = (z + away + 2 * i) % 8
         piece = zz // 2
         slot = away * 4 + i
+        wide = pl.ds(0, PARTS[k][1])
         return pltpu.make_async_remote_copy(
-            src_ref=ZS.at[k, piece // 2, piece % 2], dst_ref=ZR.at[k, slot], send_sem=ss.at[zk[k] + i],
+            src_ref=ZS.at[k, piece // 2, piece % 2, :, wide], dst_ref=ZR.at[k, slot, :, wide], send_sem=ss.at[zk[k] + i],
             recv_sem=rs.at[zk[k] + slot], device_id=dev(dz=away + 2 * i), device_id_type=MESH,
         )
 
     def r3(k):
+        n = PARTS[k][1]
+        wide = pl.ds(0, n)
         for cp in ra2[k]:
             cp.wait_recv()
-        total = PA[k, dz0, dc0]
+        total = PA[k, dz0, dc0, :, wide]
         for i in range(3):
-            total += RA2[k, i].astype(F32)
-        ZS[k, 0] = total.astype(BF16).reshape(2, 16, QUART)
+            total += RA2[k, i, :, wide].astype(F32)
+        ZS[k, 0, :, :, wide] = total.astype(BF16).reshape(2, 16, n)
         for cp in rb2[k]:
             cp.wait_recv()
-        total = PB[k, 0, 0, 0]
+        total = PB[k, 0, 0, 0, :, wide]
         for i in range(3):
-            total += RB2[k, i].astype(F32)
-        ZS[k, 1] = total.astype(BF16).reshape(2, 16, QUART)
+            total += RB2[k, i, :, wide].astype(F32)
+        ZS[k, 1, :, :, wide] = total.astype(BF16).reshape(2, 16, n)
         zk[k], gk[k] = counter[0], counter[0] + 8
         counter[0] += 24
         for i in range(1, 4):
@@ -470,36 +486,39 @@
             z_copy(k, 0).start()
 
     def o_copy(k, dx, i):
-        part = FZ.at[k]
+        wide = pl.ds(0, PARTS[k][1])
         return pltpu.make_async_remote_copy(
-            src_ref=part, dst_ref=OUT.at[k, c, zh // 2, zh % 2], send_sem=ss.at[gk[k] + dx * 4 + i],
+            src_ref=FZ.at[k, :, wide], dst_ref=OUT.at[k, c, zh // 2, zh % 2, :, wide], send_sem=ss.at[gk[k] + dx * 4 + i],
             recv_sem=rs.at[gk[k] + c * 4 + zh], device_id=dev(dx, 0, 2 * i, tok_core + c), device_id_type=MESH,
         )
 
     def r4(k):
+        first, n = PARTS[k]
+        wide = pl.ds(0, n)
+
         @pl.when(away == 0)
         def _():
             for slot in range(1, 8):
                 pltpu.make_async_remote_copy(
-                    src_ref=ZR.at[k, slot], dst_ref=ZR.at[k, slot], send_sem=ss.at[zk[k]],
+                    src_ref=ZR.at[k, slot, :, wide], dst_ref=ZR.at[k, slot, :, wide], send_sem=ss.at[zk[k]],
                     recv_sem=rs.at[zk[k] + slot], device_id=dev(dz=1), device_id_type=MESH,
                 ).wait_recv()
             ab, rh = zh // 2, zh % 2
-            acc = ZS[k, ab, rh].astype(F32)
+            acc = ZS[k, ab, rh, :, wide].astype(F32)
             for slot in range(1, 8):
-                acc += ZR[k, slot].astype(F32)
+                acc += ZR[k, slot, :, wide].astype(F32)
             row = META[0, 0, dc0, 3:4, :]
             lanes = lax.broadcasted_iota(jnp.int32, (16, 128), 1)
             picks = lanes == lax.broadcasted_iota(jnp.int32, (16, 128), 0) + 16 * rh
             delta16 = jnp.sum(jnp.where(picks, row, 0.0), axis=1, keepdims=True)
-            wide = VW[:, pl.ds(align(c * HALF + ab * W + k * QUART), QUART)]
-            FZ[k] = (acc + delta16 * wide).astype(BF16)
+            weight = VW[:, pl.ds(align(c * HALF + ab * W + first), n)]
+            FZ[k, :, wide] = (acc + delta16 * weight).astype(BF16)
             for dx, i in others:
                 o_copy(k, dx, i).start()
 
             @pl.when(tok_core == c)
             def _():
-                OUT[k, c, ab, rh] = FZ[k]
+                OUT[k, c, ab, rh, :, wide] = FZ[k, :, wide]
 
             @pl.when(tok_core != c)
             def _():
@@ -508,9 +527,12 @@
     home = (zl * 2 + c) == x
 
     def r6(k):
+        first, n = PARTS[k]
+        wide = pl.ds(0, n)
+
         def o_wait(core, piece):
             pltpu.make_async_remote_copy(
-                src_ref=FZ.at[k], dst_ref=OUT.at[k, core, piece // 2, piece % 2], send_sem=ss.at[gk[k]],
+                src_ref=FZ.at[k, :, wide], dst_ref=OUT.at[k, core, piece // 2, piece % 2, :, wide], send_sem=ss.at[gk[k]],
                 recv_sem=rs.at[gk[k] + core * 4 + piece], device_id=dev(dx=1), device_id_type=MESH,
             ).wait_recv()
 
@@ -525,9 +547,9 @@
 
         for cs in range(2):
             for ab in range(2):
-                at = cs * HALF + ab * W + k * QUART
+                at = cs * HALF + ab * W + first
                 for rh in range(2):
-                    gh[rh * 16 : (rh + 1) * 16, at : at + QUART] = OUT[k, cs, ab, rh]
+                    gh[rh * 16 : (rh + 1) * 16, at : at + n] = OUT[k, cs, ab, rh, :, wide]
 
     vocab = (offset + lax.broadcasted_iota(jnp.int32, (VOC, 1), 0)).astype(F32)
     LK[...] = (token == vocab).astype(BF16)
@@ -539,18 +561,24 @@
         looked = jnp.dot(LK[...], C[:, :, :, :, at].reshape(TOK, PIECE), preferred_element_type=F32)
         ge[:, at] = (head + normalizer * looked).astype(BF16)
 
-    p1(0)
-    r1(0)
-    p1(1)
+    p1a(0)
+    r1a(0)
+    p1b(0)
+    r1b(0)
+    p1a(1)
+    p1b(1)
     gat_c.s4(1)
-    r1(1)
-    p1(2)
+    r1a(1)
+    r1b(1)
+    p1a(2)
+    p1b(2)
     gat_c.s4(2)
     gat_c.s4z(0)
     vv[2].wait_recv()
     value_step(3, dev(dy=2))
     r2(0)
-    r1(2)
+    r1a(2)
+    r1b(2)
     gat_c.s4z(1)
     gat_c.s5(0)
     embed(0)
@@ -623,20 +651,20 @@
             V((VOC, TOK), F32),
             V((VOC, TOK), BF16),
             V((4, 2, 2, ROWS, 2 * VOC), BF16),
-            V((3, 2, 2, ROWS, QUART), F32),
-            V((3, 4, 2, 2, ROWS, QUART), F32),
-            V((3, 4, 2, 2, ROWS, QUART), BF16),
-            V((3, 4, 2, 2, ROWS, QUART), BF16),
-            V((3, 3, 2, 2, ROWS, QUART), BF16),
-            V((3, 3, 4, ROWS, QUART), BF16),
-            V((3, 2, 2, ROWS, QUART), BF16),
-            V((3, 4, ROWS, QUART), BF16),
-            V((3, 3, ROWS, QUART), BF16),
-            V((3, 3, ROWS, QUART), BF16),
-            V((3, 2, 2, 16, QUART), BF16),
-            V((3, 8, 16, QUART), BF16),
-            V((3, 16, QUART), BF16),
-            V((3, 2, 2, 2, 16, QUART), BF16),
+            V((3, 2, 2, ROWS, WIDE), F32),
+            V((3, 4, 2, 2, ROWS, WIDE), F32),
+            V((3, 4, 2, 2, ROWS, WIDE), BF16),
+            V((3, 4, 2, 2, ROWS, WIDE), BF16),
+            V((3, 3, 2, 2, ROWS, WIDE), BF16),
+            V((3, 3, 4, ROWS, WIDE), BF16),
+            V((3, 2, 2, ROWS, WIDE), BF16),
+            V((3, 4, ROWS, WIDE), BF16),
+            V((3, 3, ROWS, WIDE), BF16),
+            V((3, 3, ROWS, WIDE), BF16),
+            V((3, 2, 2, 16, WIDE), BF16),
+            V((3, 8, 16, WIDE), BF16),
+            V((3, 16, WIDE), BF16),
+            V((3, 2, 2, 2, 16, WIDE), BF16),
             V((4, 2, 2, 8, 128), F32),
             V((2, TOK), F32),
             V((16, 2, TOK), F32),

time: 92.5 us -> 91.5 us (0.989)
  Pallas kernels: 87.9 us -> 86.6 us
    pallas_call x1, Pallas kernels: 87.9 us -> 86.6 us  [local(): pl.pallas_call(kernel, out_shape=(pltpu.VMEM((VOC, D), BF16), pltpu.VMEM(...]
where the time goes in v4:
time: 91.5 us; the launch traced here: 91.1 us
  Pallas kernels  86.6 us (95%)
  local copies, waits for them, and re-layouts  3.9 us (4%)
    pallas_call x1, Pallas kernels, local(): pl.pallas_call(kernel, out_shape=(pltpu.VMEM((VOC, D), BF16), pltpu.VMEM(...  86.6 us
    unnamed x3, local copies, waits for them, and re-layouts  3.9 us

profile of v4, /device:TPU:32, one launch (start us, length us, event | category | flops | bytes accessed | tf_op | source)
XLA Modules:
  0.0 91.1 jit_solution(12093185762168430385)
XLA Ops:
  0.6 86.6 %policy_head.1 = (bf16[640,4608]{1,0:T(8,128)(2,1)S(1)}, bf16[32,4608]{1,0:T(8,128)(2,1)S(1)}, f32[36,128]{1,0:T(8,128)S(1)}) custom-call(bf16[32,4608]{1,0:T(8,128)(2,1)} %hs.1, bf16[640,4608]{1,0:T(8,128)(2,1)} %emb.1, s32[1,32]{1,0:T(1,128)} %bitcast.8, s32[1,32]{1,0:T(1,128)} %bitcast.9, bf16[1,32]{1,0:T(2,128)(2,1)} %bitcast.10, bf16[32,4608]{1,0:T(8,128)(2,1)} %cot.1, ...), custom_call_target="tpu_custom_call" | custom-call | tf_op jit(solution)/shard_map/policy_head/pallas_call | solution.py:637
  87.2 2.6 %copy.14 = bf16[640,4608]{1,0:T(8,128)(2,1)} copy(bf16[640,4608]{1,0:T(8,128)(2,1)S(1)} %get-tuple-element.9) | data formatting | bytes 11796480
  89.8 0.6 copy.16
  90.4 0.7 copy.15
